TPU v7x, 32 devices: a whole 2x2x4 slice. The times are simulated.
32 devices in a mesh: pairs: 2 (over x), src: 8 (over z, y), tgt: 2 (over core).
Axes of the slice: x: 2, y: 2, z: 4, core: 2. Of those that a mesh axis runs over, the one named last changes fastest.
Arguments:
- src_feat: float32 [2048, 32], P(('pairs', 'src'), 'tgt'), parts along dimension 0, may hold values from -0.72 to 0.72
- tgt_feat: float32 [32768, 32], P(('pairs', 'tgt'), 'src'), parts along dimension 0, may hold values from -0.72 to 0.72
- tgt_dual: float32 [32768], P(('pairs', 'tgt')), parts along dimension 0, may hold values from -6 to 6
- core_matrix: float32 [68, 34], P('pairs'), parts along dimension 0, may hold values from -3 to 3
Outputs:
- src_dual: float32 [2048], P(('pairs', 'src')), parts along dimension 0
- tgt_dual_out: float32 [32768], P(('pairs', 'tgt')), parts along dimension 0
- core_out: float32 [68, 34], P('pairs'), parts along dimension 0
There are 2 independent parts, one for each index of `pairs`. A program takes and returns all parts, laid end to end along the dimension named above; each array names one. Nothing has to cross between parts.
All inputs are finite; a program needn't handle non-finite values.
Results may differ from a plain program's by a relative error of at most 0.0003.
Values sent between devices are 32-bit elements; how exact they have to be, the bound alone decides.
A program may use at most 64 MiB of HBM per device.

v0:
```python
import jax
import jax.numpy as jnp
from jax import lax
from jax.sharding import PartitionSpec as P

OUTER = 2


EPSILON = 0.02
HIGH = lax.Precision.HIGHEST


def merged(array, axis, combine):
    everything = jax.tree.map(lambda part: lax.all_gather(part, axis), array)
    leading = jax.tree.map(lambda part: part[0], everything)

    def step(k, so_far):
        return combine(so_far, jax.tree.map(lambda part: part[k], everything))

    return lax.fori_loop(1, lax.axis_size(axis), step, leading)


def lifted(values):
    squares = jnp.sum(values * values, axis=1, keepdims=True)
    ones = jnp.ones_like(squares)
    left = jnp.concatenate([squares, ones, -2.0 * values], axis=1)
    right = jnp.concatenate([ones, squares, values], axis=1)
    return (left, right)


def merge_logsum(earlier, later):
    top = jnp.maximum(earlier[0], later[0])
    return (top, earlier[1] * jnp.exp(earlier[0] - top) + later[1] * jnp.exp(later[0] - top))


def shards(src_feat, tgt_feat, tgt_dual, core_matrix):
    src_rows = lax.all_gather(src_feat, "tgt", axis=1, tiled=True)
    tgt_rows = lax.all_gather(tgt_feat, "src", axis=1, tiled=True)
    src_left, src_right = lifted(src_rows)
    tgt_left, tgt_right = lifted(tgt_rows)
    src_count = lax.axis_size("src")
    tgt_count = lax.axis_size("tgt")
    row_count = src_rows.shape[0]
    col_count = tgt_rows.shape[0]
    log_src = -jnp.log(jnp.float32(row_count * src_count))
    log_tgt = -jnp.log(jnp.float32(col_count * tgt_count))
    src_dual = jnp.zeros((row_count,), jnp.float32)
    for outer_step in range(OUTER):
        projected = jnp.dot(src_left, core_matrix, precision=HIGH)
        linear = jnp.dot(projected, tgt_right.T, precision=HIGH)
        row_logits = (tgt_dual[None, :] - linear) / EPSILON
        row_max = jnp.max(row_logits, axis=1)
        row_total = jnp.sum(jnp.exp(row_logits - row_max[:, None]), axis=1)
        row_max, row_total = merged((row_max, row_total), "tgt", merge_logsum)
        src_dual = EPSILON * log_src - EPSILON * (row_max + jnp.log(row_total))
        col_logits = (src_dual[:, None] - linear) / EPSILON
        col_max = jnp.max(col_logits, axis=0)
        col_exp = jnp.exp(col_logits - col_max[None, :])
        col_total = jnp.sum(col_exp, axis=0)
        piece_max, piece_total = (
            lax.all_to_all(col_max[None, :], "src", split_axis=1, concat_axis=0, tiled=True),
            lax.all_to_all(col_total[None, :], "src", split_axis=1, concat_axis=0, tiled=True),
        )
        whole_max = jnp.max(piece_max, axis=0)
        whole_total = jnp.sum(piece_total * jnp.exp(piece_max - whole_max[None, :]), axis=0)
        dual_piece = EPSILON * log_tgt - EPSILON * (whole_max + jnp.log(whole_total))
        tgt_dual = lax.all_gather(dual_piece, "src", axis=0, tiled=True)
        coupling = jnp.exp((src_dual[:, None] + tgt_dual[None, :] - linear) / EPSILON)
        weighted = jnp.dot(coupling, tgt_left, precision=HIGH)
        core_part = jnp.dot(src_right.T, weighted, precision=HIGH)
        core_matrix = -2.0 * lax.psum(core_part, ("src", "tgt"))
    return (src_dual, tgt_dual, core_matrix)


def solution(mesh):
    placed = (
        P(("pairs", "src"), "tgt"),
        P(("pairs", "tgt"), "src"),
        P(("pairs", "tgt")),
        P("pairs", None),
    )
    return jax.shard_map(
        shards,
        mesh=mesh,
        in_specs=placed,
        out_specs=(P(("pairs", "src")), P(("pairs", "tgt")), P("pairs", None)),
        check_vma=False,
    )
```

profile of v0, /device:TPU:0, one launch (start us, length us, event | category | flops | bytes accessed | tf_op | source)
XLA Modules:
  0.0 311.4 jit_solution(1951934580604606527)
XLA Ops:
  7.2 0.0 copy-start
  7.2 0.0 copy-start.3
  7.2 0.0 all-gather.11.cloned.1.call-start
  7.2 0.7 all-gather.11.cloned.1.call-update
  7.9 2.2 all_gather.36
  10.1 0.0 copy-done
  10.1 0.3 fusion.32
  10.4 42.7 %all-gather.11.cloned.1.call-done = f32[8,4,8192]{2,1,0:T(4,128)} async-done(((f32[1,4,8192]{2,1,0:T(4,128)}), f32[8,4,8192]{2,1,0:T(4,128)}) %all-gather.11.cloned.1.call-update) | async-done | bytes 1048592 | tf_op jit(solution)/shard_map/all_gather | solution.py:38
  53.1 1.6 reshape.132
  54.7 0.2 broadcast_multiply_fusion
  54.9 0.0 copy-done.3
  54.9 3.8 %fusion.10 = (f32[128]{0:T(128)S(1)}, f32[128,8192]{1,0:T(8,128)S(1)}) fusion(f32[8192]{0:T(1024)S(1)} %copy-done.3, f32[128,34]{1,0:T(8,128)S(1)} %fusion.32, f32[8192,32]{0,1:T(8,128)S(1)} %bitcast.89, f32[8192,1]{0,1:T(1,128)S(1)} %bitcast.91, f32[8192,1]{0,1:T(1,128)S(1)} %broadcast_in_dim.10), kind=kOutput, calls=%fused_computation.18 | convolution fusion | flops 431521664 | bytes 5359104 | tf_op jit(solution)/shard_map/dot_general | solution.py:50
  58.7 0.0 copy-start.2
  58.7 1.0 exponential_reduce_fusion.3
  59.7 1.8 all-gather.6
  61.5 1.8 all-gather.5
  63.2 1.2 fusion.11
  64.4 0.0 copy-done.2
  64.4 3.4 %all-to-all-start = ((f32[1,8,1024]{2,0,1:T(1,128)}), f32[1,8,1024]{2,0,1:T(1,128)S(1)}, u32[]{:S(2)}, u32[]{:S(2)}) async-start(f32[1,8,1024]{2,0,1:T(1,128)} %bitcast.11), calls=%async_computation | async-start | bytes 65536 | tf_op jit(solution)/shard_map/all_to_all | solution.py:61
  67.8 3.7 %exponential_reduce_fusion.2 = f32[8192]{0:T(1024)} fusion(f32[128,8192]{1,0:T(8,128)} %copy-done.2, f32[8192]{0:T(1024)} %fusion.11, f32[128]{0:T(128)S(1)} %multiply_subtract_fusion.3), kind=kLoop, calls=%fused_computation.14 | loop fusion | flops 4186112 | bytes 4260352 | tf_op jit(solution)/shard_map/reduce_sum | solution.py:59
  71.5 3.0 all-to-all-done
  74.5 3.3 %all-to-all-start.1 = ((f32[1,8,1024]{2,0,1:T(1,128)}), f32[1,8,1024]{2,0,1:T(1,128)S(1)}, u32[]{:S(2)}, u32[]{:S(2)}) async-start(f32[1,8,1024]{2,0,1:T(1,128)} %bitcast.12), calls=%async_computation.1 | async-start | bytes 65536 | tf_op jit(solution)/shard_map/all_to_all | solution.py:62
  77.8 6.6 %all-to-all-done.1 = f32[1,8,1024]{2,0,1:T(1,128)S(1)} async-done(((f32[1,8,1024]{2,0,1:T(1,128)}), f32[1,8,1024]{2,0,1:T(1,128)S(1)}, u32[]{:S(2)}, u32[]{:S(2)}) %all-to-all-start.1) | async-done | bytes 32800 | tf_op jit(solution)/shard_map/all_to_all | solution.py:62
  84.5 30.4 %all_gather.42 = f32[8192]{0:T(1024)S(1)} all-gather(f32[1024]{0:T(1024)S(1)} %multiply_subtract_fusion.1), channel_id=1, replica_groups=mesh['pairs'=2,'src'=8,'tgt'=2] {'src'}, dimensions={0}, use_global_device_ids=true | all-gather | bytes 36864 | tf_op jit(solution)/shard_map/all_gather | solution.py:67
  114.9 6.2 %fusion.5 = f32[128,34]{1,0:T(8,128)S(1)} fusion(f32[128,8192]{1,0:T(8,128)} %copy-done.2, f32[8192]{0:T(1024)S(1)} %all_gather.42, f32[128]{0:T(128)S(1)} %multiply_subtract_fusion.3, f32[8192,32]{0,1:T(8,128)S(1)} %get-tuple-element.27, f32[8192,1]{0,1:T(1,128)S(1)} %broadcast_in_dim.10, f32[8192,1]{0,1:T(1,128)S(1)} %bitcast.92), kind=kOutput, calls=%fused_computation.9 | convolution fusion | flops 431521792 | bytes 5359104 | tf_op jit(solution)/shard_map/dot_general | solution.py:69
  121.1 0.2 fusion.31
  121.3 57.8 %psum.14 = f32[34,34]{1,0:T(8,128)S(1)} all-reduce(f32[34,34]{1,0:T(8,128)S(1)} %fusion.31), channel_id=1, replica_groups=mesh['pairs'=2,'src'=8,'tgt'=2] {'src','tgt'}, use_global_device_ids=true, to_apply=%region_8.0 | all-reduce | flops 1156 | bytes 9248 | tf_op jit(solution)/shard_map/psum | solution.py:71
  179.1 0.3 fusion.28
  179.4 3.8 %fusion.12 = (f32[128]{0:T(128)S(1)}, f32[128,8192]{1,0:T(8,128)S(1)}) fusion(f32[8192]{0:T(1024)S(1)} %all_gather.42, f32[128,34]{1,0:T(8,128)S(1)} %fusion.28, f32[8192,32]{0,1:T(8,128)S(1)} %bitcast.90, f32[8192,1]{0,1:T(1,128)S(1)} %bitcast.93, f32[8192,1]{0,1:T(1,128)S(1)} %broadcast_in_dim.10), kind=kOutput, calls=%fused_computation.20 | convolution fusion | flops 431521664 | bytes 5359104 | tf_op jit(solution)/shard_map/dot_general | solution.py:50
  183.2 0.0 copy-start.1
  183.2 1.0 exponential_reduce_fusion.1
  184.2 1.8 all-gather.8
  186.0 1.8 all-gather.7
  187.8 0.0 copy-start.4
  187.8 1.1 fusion.13
  188.9 0.0 copy-done.1
  188.9 3.3 %all-to-all-start.2 = ((f32[1,8,1024]{2,0,1:T(1,128)}), f32[1,8,1024]{2,0,1:T(1,128)S(1)}, u32[]{:S(2)}, u32[]{:S(2)}) async-start(f32[1,8,1024]{2,0,1:T(1,128)} %bitcast.19), calls=%async_computation.2 | async-start | bytes 65536 | tf_op jit(solution)/shard_map/all_to_all | solution.py:61
  192.3 3.7 %exponential_reduce_fusion = f32[8192]{0:T(1024)} fusion(f32[128,8192]{1,0:T(8,128)} %copy-done.1, f32[8192]{0:T(1024)} %fusion.13, f32[128]{0:T(128)S(1)} %multiply_subtract_fusion.2), kind=kLoop, calls=%fused_computation.5 | loop fusion | flops 4186112 | bytes 4260352 | tf_op jit(solution)/shard_map/reduce_sum | solution.py:59
  196.0 2.9 all-to-all-done.2
  198.9 3.3 %all-to-all-start.3 = ((f32[1,8,1024]{2,0,1:T(1,128)}), f32[1,8,1024]{2,0,1:T(1,128)S(1)}, u32[]{:S(2)}, u32[]{:S(2)}) async-start(f32[1,8,1024]{2,0,1:T(1,128)} %bitcast.20), calls=%async_computation.3 | async-start | bytes 65536 | tf_op jit(solution)/shard_map/all_to_all | solution.py:62
  202.3 6.6 %all-to-all-done.3 = f32[1,8,1024]{2,0,1:T(1,128)S(1)} async-done(((f32[1,8,1024]{2,0,1:T(1,128)}), f32[1,8,1024]{2,0,1:T(1,128)S(1)}, u32[]{:S(2)}, u32[]{:S(2)}) %all-to-all-start.3) | async-done | bytes 32800 | tf_op jit(solution)/shard_map/all_to_all | solution.py:62
  208.9 30.4 %all_gather.47 = f32[8192]{0:T(1024)S(1)} all-gather(f32[1024]{0:T(1024)S(1)} %multiply_subtract_fusion), channel_id=1, replica_groups=mesh['pairs'=2,'src'=8,'tgt'=2] {'src'}, dimensions={0}, use_global_device_ids=true | all-gather | bytes 36864 | tf_op jit(solution)/shard_map/all_gather | solution.py:67
  239.3 0.0 copy-done.4
  239.3 6.2 %fusion = f32[128,34]{1,0:T(8,128)S(1)} fusion(f32[128,8192]{1,0:T(8,128)} %copy-done.1, f32[8192]{0:T(1024)S(1)} %all_gather.47, f32[128]{0:T(128)S(1)} %multiply_subtract_fusion.2, f32[8192,32]{0,1:T(8,128)S(1)} %get-tuple-element.27, f32[8192,1]{0,1:T(1,128)S(1)} %broadcast_in_dim.10, f32[8192,1]{0,1:T(1,128)S(1)} %bitcast.94), kind=kOutput, calls=%fused_computation | convolution fusion | flops 431521792 | bytes 5359104 | tf_op jit(solution)/shard_map/dot_general | solution.py:69
  245.5 0.2 fusion.30
  245.7 57.6 %psum.15 = f32[34,34]{1,0:T(8,128)S(1)} all-reduce(f32[34,34]{1,0:T(8,128)S(1)} %fusion.30), channel_id=1, replica_groups=mesh['pairs'=2,'src'=8,'tgt'=2] {'src','tgt'}, use_global_device_ids=true, to_apply=%region_15.0 | all-reduce | flops 1156 | bytes 9248 | tf_op jit(solution)/shard_map/psum | solution.py:71
  303.4 0.6 broadcast_multiply_fusion.1
  304.0 0.6 copy.16
  (11 shorter events, 0.2 us)
Async XLA Ops:
  7.2 2.9 copy-start
  7.2 47.7 %copy-start.3 = (f32[8192]{0:T(1024)S(1)}, f32[8192]{0:T(1024)}, u32[]{:S(2)}) copy-start(f32[8192]{0:T(1024)} %param.6) | copy-start | bytes 98308
  7.2 45.9 %all-gather.11.cloned.1.call-start = ((), (), s32[]{:S(2)}) async-start(), calls=%async_computation.4 | async-start | bytes 1179648 | tf_op jit(solution)/shard_map/all_gather | solution.py:38
  58.7 5.7 %copy-start.2 = (f32[128,8192]{1,0:T(8,128)}, f32[128,8192]{1,0:T(8,128)S(1)}, u32[]{:S(2)}) copy-start(f32[128,8192]{1,0:T(8,128)S(1)} %get-tuple-element.38) | copy-start | bytes 12582916
  64.4 10.1 %all-to-all-start = ((f32[1,8,1024]{2,0,1:T(1,128)}), f32[1,8,1024]{2,0,1:T(1,128)S(1)}, u32[]{:S(2)}, u32[]{:S(2)}) async-start(f32[1,8,1024]{2,0,1:T(1,128)} %bitcast.11), calls=%async_computation | async-start | bytes 65536 | tf_op jit(solution)/shard_map/all_to_all | solution.py:61
  74.5 10.0 %all-to-all-start.1 = ((f32[1,8,1024]{2,0,1:T(1,128)}), f32[1,8,1024]{2,0,1:T(1,128)S(1)}, u32[]{:S(2)}, u32[]{:S(2)}) async-start(f32[1,8,1024]{2,0,1:T(1,128)} %bitcast.12), calls=%async_computation.1 | async-start | bytes 65536 | tf_op jit(solution)/shard_map/all_to_all | solution.py:62
  183.2 5.7 %copy-start.1 = (f32[128,8192]{1,0:T(8,128)}, f32[128,8192]{1,0:T(8,128)S(1)}, u32[]{:S(2)}) copy-start(f32[128,8192]{1,0:T(8,128)S(1)} %get-tuple-element.40) | copy-start | bytes 12582916
  187.8 51.6 %copy-start.4 = (f32[128]{0:T(128)}, f32[128]{0:T(128)S(1)}, u32[]{:S(2)}) copy-start(f32[128]{0:T(128)S(1)} %multiply_subtract_fusion.2) | copy-start | bytes 1540
  188.9 10.0 %all-to-all-start.2 = ((f32[1,8,1024]{2,0,1:T(1,128)}), f32[1,8,1024]{2,0,1:T(1,128)S(1)}, u32[]{:S(2)}, u32[]{:S(2)}) async-start(f32[1,8,1024]{2,0,1:T(1,128)} %bitcast.19), calls=%async_computation.2 | async-start | bytes 65536 | tf_op jit(solution)/shard_map/all_to_all | solution.py:61
  198.9 10.0 %all-to-all-start.3 = ((f32[1,8,1024]{2,0,1:T(1,128)}), f32[1,8,1024]{2,0,1:T(1,128)S(1)}, u32[]{:S(2)}, u32[]{:S(2)}) async-start(f32[1,8,1024]{2,0,1:T(1,128)} %bitcast.20), calls=%async_computation.3 | async-start | bytes 65536 | tf_op jit(solution)/shard_map/all_to_all | solution.py:62
Sparse Core Ops, SparseCore 0:
  10.2 42.9 all-gather.10
where the time goes:
time: 312 us; the launch traced here: 311 us
  blocking collectives  185 us (59%)
  waiting for transfers between devices  62.4 us (20%)
  matrix products  21 us (7%)
  between operations  14.2 us (5%)
  starting transfers between devices  13.4 us (4%)
  other arithmetic  12.7 us (4%)
    psum x2, blocking collectives, shards(): core_matrix = -2.0 * lax.psum(core_part, ('src', 'tgt'))  115 us
    all_gather x2, blocking collectives, shards(): tgt_dual = lax.all_gather(dual_piece, 'src', axis=0, tiled=True)  60.8 us
    all_gather x1, waiting for transfers between devices, shards(): tgt_rows = lax.all_gather(tgt_feat, 'src', axis=1, tiled=True)  42.7 us
    all_to_all x2, waiting for transfers between devices, shards(): lax.all_to_all(col_total[None, :], 'src', split_axis=1, concat_axis=0, ti...  13.2 us
    dot_general x2, matrix products, shards(): weighted = jnp.dot(coupling, tgt_left, precision=HIGH)  12.4 us
    dot_general x2, matrix products, shards(): linear = jnp.dot(projected, tgt_right.T, precision=HIGH)  7.61 us
    reduce_sum x2, other arithmetic, shards(): col_total = jnp.sum(col_exp, axis=0)  7.45 us
    all_gather x4, blocking collectives, merged(): everything = jax.tree.map(lambda part: lax.all_gather(part, axis), array)  7.03 us
  transfers between devices with their start and end apart: 5, of which 5 were waited for; matrix products, arithmetic and copies ran while one was open for 3% of the time, Pallas kernels for 0%

commit v1 on v0

v1 whole, which is shorter than its diff:
```python
import functools
import math

import jax
import jax.numpy as jnp
from jax import lax
from jax.experimental import pallas as pl
from jax.experimental.pallas import tpu as pltpu
from jax.sharding import PartitionSpec as P

OUTER = 2
EPSILON = 0.02
LOG2E = math.log2(math.e)
UNIT = EPSILON / LOG2E
LANES = 128
MESH = pl.DeviceIdType.MESH
BF16 = jnp.bfloat16
F32 = jnp.float32


def split3(x):
    high = x.astype(BF16).astype(F32)
    rest = x - high
    mid = rest.astype(BF16).astype(F32)
    return high, mid, rest - mid


def lanes_below(x, count):
    return jnp.where(lax.broadcasted_iota(jnp.int32, x.shape, 1) < count, x, 0.0)


def shifted(x, by):
    return x if by % LANES == 0 else pltpu.roll(x, by % LANES, 1)


def kernel(
    dims, src_ref, tgt_ref, dual_ref, core_ref, u_out, g_out, core_out,
    srcbuf, tgtbuf, lsebuf, corebuf, gbuf, sl, sr, tl, tr, sls, srs, tls, trt, sps, logits, gcol, weighted, urow, square,
    send_sem, recv_sem,
):
    S, T, rows, cols, fs, ft, feat, ns, nt = dims
    D = S * T
    rank = feat + 2
    st = -(-rank // 8) * 8
    jr = cols // LANES
    nr = rows // LANES
    s, t = lax.axis_index("src"), lax.axis_index("tgt")
    me = s * T + t

    def everyone(act):
        def body(k, unused):
            peer = lax.rem(me + k, D)
            act(peer, peer // T, lax.rem(peer, T))
            return unused

        lax.fori_loop(1, D, body, 0)

    def column(act):
        def body(k, unused):
            act(lax.rem(s + k, S))
            return unused

        lax.fori_loop(1, S, body, 0)

    def remote(phase, src, dst, out_id, in_id, device):
        return pltpu.make_async_remote_copy(
            src_ref=src, dst_ref=dst, send_sem=send_sem.at[phase, out_id], recv_sem=recv_sem.at[phase, in_id],
            device_id=device, device_id_type=MESH,
        )

    def share(phase, buf, k):
        def act(peer, ps, pt):
            remote(phase, buf.at[k, me], buf.at[k, me], peer, me, {"src": ps, "tgt": pt}).start()

        everyone(act)

    def shared(phase, buf, k):
        def act(peer, ps, pt):
            remote(phase, buf.at[k, peer], buf.at[k, peer], peer, peer, {"src": ps, "tgt": pt}).wait_recv()

        everyone(act)

    def sent(phase, buf, k):
        def act(peer, ps, pt):
            remote(phase, buf.at[k, me], buf.at[k, me], peer, me, {"src": ps, "tgt": pt}).wait_send()

        everyone(act)

    barrier = pltpu.get_barrier_semaphore()

    def greet(peer, ps, pt):
        pl.semaphore_signal(barrier, inc=1, device_id={"src": ps, "tgt": pt}, device_id_type=MESH)

    everyone(greet)
    srcbuf[s, t] = src_ref[...]
    tgtbuf[s] = tgt_ref[s]
    own_dual = dual_ref[s] * (1.0 / UNIT)
    for r in range(jr):
        gcol[r * LANES : (r + 1) * LANES, :] = jnp.broadcast_to(own_dual[r : r + 1, :], (LANES, LANES)).T
    square[...] = jnp.zeros_like(square)
    square[:rank, :rank] = core_ref[...]
    turned = square[...].T[:st, :]
    pl.semaphore_wait(barrier, D - 1)

    def send_tgt(ps):
        remote(1, tgt_ref.at[ps], tgtbuf.at[s], ps, s, {"src": ps}).start()

    column(send_tgt)

    def send_src(peer, ps, pt):
        remote(0, src_ref, srcbuf.at[s, t], peer, me, {"src": ps, "tgt": pt}).start()

    everyone(send_src)

    def get_tgt(ps):
        remote(1, tgt_ref.at[ps], tgtbuf.at[ps], ps, ps, {"src": ps}).wait_recv()

    column(get_tgt)

    def lift(left, right):
        values = right[2:rank, :]
        squares = jnp.sum(values * values, axis=0, keepdims=True)
        ones = jnp.ones_like(squares)
        left[rank:, :] = jnp.zeros_like(left[rank:, :])
        right[rank:, :] = jnp.zeros_like(right[rank:, :])
        left[0:1, :] = squares
        left[1:2, :] = ones
        left[2:rank, :] = -2.0 * values
        right[0:1, :] = ones
        right[1:2, :] = squares

    def stacked(parts, height):
        width = parts[0].shape[1]
        fill = height - st * len(parts)
        return jnp.concatenate(list(parts) + ([jnp.zeros((fill, width), F32)] if fill else []), axis=0)

    deep = trt.shape[1]
    wide = srs.shape[1]
    for k in range(S):
        for r in range(jr):
            tr[2 + k * ft : 2 + (k + 1) * ft, r * LANES : (r + 1) * LANES] = tgtbuf[k, r * ft : (r + 1) * ft, :]
    lift(tl, tr)
    t0, t1, t2 = split3(tr[...])
    trt[...] = stacked((t0, t1, t0, t1, t2, t0), deep).T.astype(BF16)
    tls[...] = stacked(split3(tl[...]), wide).astype(BF16)

    def get_src(peer, ps, pt):
        remote(0, src_ref, srcbuf.at[ps, pt], peer, peer, {"src": ps, "tgt": pt}).wait_recv()

    everyone(get_src)
    for k in range(S):
        for h in range(T):
            sr[2 + h * fs : 2 + (h + 1) * fs, k * rows : (k + 1) * rows] = srcbuf[k, h]
    lift(sl, sr)
    sls[...] = stacked(split3(sl[...]), wide).astype(BF16)
    srs[...] = stacked(split3(sr[...]), wide).T.astype(BF16)

    per = LANES // st
    block = min(256, ns)
    chunk = min(256, cols)
    for step in range(OUTER):
        k0, k1, k2 = split3(turned * (-1.0 / UNIT))
        lhs = stacked(
            (k0 + shifted(k0, st) + shifted(k0, 2 * st), k1 + shifted(k1, st), k2), 3 * st
        ).astype(BF16)
        proj = jnp.dot(lhs, sls[...], preferred_element_type=F32)
        proj = proj[:st] + (proj[st : 2 * st] + proj[2 * st :])
        p0, p1, p2 = split3(proj)
        sps[...] = stacked((p0, p0, p1, p1, p0, p2), deep).astype(BF16)
        for b in range(ns // block):
            part = jnp.dot(trt[...], sps[:, b * block : (b + 1) * block], preferred_element_type=F32)
            for h in range(block // LANES):
                at = b * block // LANES + h
                here = part[:, h * LANES : (h + 1) * LANES] + gcol[...]
                logits[:, at * LANES : (at + 1) * LANES] = here
                top = jnp.max(here, axis=0, keepdims=True)
                total = jnp.sum(jnp.exp2(here - top), axis=0, keepdims=True)
                lsebuf[step, me, at : at + 1, :] = top + jnp.log2(total)
        share(2 + 2 * step, lsebuf, step)
        shared(2 + 2 * step, lsebuf, step)
        top = jnp.max(lsebuf[step], axis=0)
        total = jnp.sum(jnp.exp2(lsebuf[step] - top[None]), axis=0)
        urow[...] = -math.log2(ns) - (top + jnp.log2(total))
        u_all = jnp.concatenate([urow[k : k + 1, :] for k in range(ns // LANES)], axis=1)
        for c in range(cols // chunk):
            sl_c = slice(c * chunk, (c + 1) * chunk)
            x = logits[sl_c, :] + u_all
            top = jnp.max(x, axis=1, keepdims=True)
            e = jnp.exp2(x - top)
            high = e.astype(BF16)
            low = (e - high.astype(F32)).astype(BF16)
            acc = jnp.dot(high, srs[...], preferred_element_type=F32) + jnp.dot(low, srs[...], preferred_element_type=F32)
            total = acc[:, 0:1]
            scaled = acc * (1.0 / total)
            first = scaled.astype(BF16)
            weighted[sl_c, :wide] = first
            weighted[sl_c, wide:] = (scaled - first.astype(F32)).astype(BF16)
            gcol[sl_c, :] = (gcol[sl_c, :] - math.log2(nt)) - (top + jnp.log2(total))
        if step == OUTER - 1:
            for r in range(jr):
                gbuf[s, r : r + 1, :] = gcol[r * LANES : (r + 1) * LANES, :].T[0:1, :] * UNIT

            def send_g(ps):
                remote(1 + 2 * OUTER + 1, gbuf.at[s], gbuf.at[s], ps, s, {"src": ps}).start()

            column(send_g)
        ext = jnp.dot(tls[...], weighted[...], preferred_element_type=F32)
        ext = ext[:, :wide] + ext[:, wide:]
        kt = ext[:st] + (ext[st : 2 * st] + ext[2 * st : 3 * st])
        kt = kt + (shifted(kt, -st) + shifted(kt, -2 * st))
        kt = lanes_below(kt * (1.0 / nt), st)
        for group in range(corebuf.shape[2] // 8):
            tile = None
            for k in range(per):
                n = group * per + k
                if n * 8 < st:
                    piece = shifted(kt[n * 8 : n * 8 + 8, :], k * st)
                    tile = piece if tile is None else tile + piece
            corebuf[step, me, group * 8 : group * 8 + 8, :] = tile
        share(3 + 2 * step, corebuf, step)
        shared(3 + 2 * step, corebuf, step)
        summed = -2.0 * jnp.sum(corebuf[step], axis=0)
        turned = jnp.concatenate(
            [
                lanes_below(shifted(summed[n // per * 8 : n // per * 8 + 8, :], -(n % per) * st), st)
                for n in range(st // 8)
            ],
            axis=0,
        )
    u_out[...] = urow[pl.ds(s * nr, nr), :] * UNIT
    square[:st, :] = turned
    core_out[...] = square[...].T[:rank, :rank]

    def get_g(ps):
        remote(1 + 2 * OUTER + 1, gbuf.at[ps], gbuf.at[ps], ps, ps, {"src": ps}).wait_recv()

    column(get_g)
    g_out[...] = gbuf[...]

    def done_tgt(ps):
        remote(1, tgt_ref.at[ps], tgtbuf.at[s], ps, s, {"src": ps}).wait_send()
        remote(1 + 2 * OUTER + 1, gbuf.at[s], gbuf.at[s], ps, s, {"src": ps}).wait_send()

    column(done_tgt)

    def done_src(peer, ps, pt):
        remote(0, src_ref, srcbuf.at[s, t], peer, me, {"src": ps, "tgt": pt}).wait_send()

    everyone(done_src)
    for step in range(OUTER):
        sent(2 + 2 * step, lsebuf, step)
        sent(3 + 2 * step, corebuf, step)


def shards(src_feat, tgt_feat, tgt_dual, core_matrix):
    S, T = lax.axis_size("src"), lax.axis_size("tgt")
    D = S * T
    rows, fs = src_feat.shape
    held, ft = tgt_feat.shape
    feat = fs * T
    cols = held // S
    ns, nt = rows * S, held * T
    rank = feat + 2
    st = -(-rank // 8) * 8
    jr, nr = cols // LANES, rows // LANES
    per = LANES // st
    groups = -(-(st // 8) // per)
    deep = -(-6 * st // LANES) * LANES
    wide = -(-3 * st // LANES) * LANES
    dims = (S, T, rows, cols, fs, ft, feat, ns, nt)
    src = src_feat.T
    tgt = tgt_feat.reshape(S * jr, LANES, ft).transpose(0, 2, 1).reshape(S, jr * ft, LANES)
    dual = tgt_dual.reshape(S, jr, LANES)
    phases = 2 + 2 * OUTER + 1
    vmem = pl.BlockSpec(memory_space=pltpu.VMEM)
    u, g, core = pl.pallas_call(
        functools.partial(kernel, dims),
        out_shape=(
            jax.ShapeDtypeStruct((nr, LANES), F32),
            jax.ShapeDtypeStruct((S, jr, LANES), F32),
            jax.ShapeDtypeStruct((rank, rank), F32),
        ),
        in_specs=[vmem] * 4,
        out_specs=(vmem,) * 3,
        scratch_shapes=[
            pltpu.VMEM((S, T, fs, rows), F32),
            pltpu.VMEM((S, jr * ft, LANES), F32),
            pltpu.VMEM((OUTER, D, ns // LANES, LANES), F32),
            pltpu.VMEM((OUTER, D, groups * 8, LANES), F32),
            pltpu.VMEM((S, jr, LANES), F32),
            pltpu.VMEM((st, ns), F32),
            pltpu.VMEM((st, ns), F32),
            pltpu.VMEM((st, cols), F32),
            pltpu.VMEM((st, cols), F32),
            pltpu.VMEM((wide, ns), BF16),
            pltpu.VMEM((ns, wide), BF16),
            pltpu.VMEM((wide, cols), BF16),
            pltpu.VMEM((cols, deep), BF16),
            pltpu.VMEM((deep, ns), BF16),
            pltpu.VMEM((cols, ns), F32),
            pltpu.VMEM((cols, LANES), F32),
            pltpu.VMEM((cols, 2 * wide), BF16),
            pltpu.VMEM((ns // LANES, LANES), F32),
            pltpu.VMEM((LANES, LANES), F32),
            pltpu.SemaphoreType.DMA((phases, D)),
            pltpu.SemaphoreType.DMA((phases, D)),
        ],
        compiler_params=pltpu.CompilerParams(
            collective_id=0, has_side_effects=True, vmem_limit_bytes=48 * 1024 * 1024
        ),
    )(src, tgt, dual, core_matrix)
    return u.reshape(rows), g.reshape(held), core


def solution(mesh):
    placed = (
        P(("pairs", "src"), "tgt"),
        P(("pairs", "tgt"), "src"),
        P(("pairs", "tgt")),
        P("pairs", None),
    )
    return jax.shard_map(
        shards,
        mesh=mesh,
        in_specs=placed,
        out_specs=(P(("pairs", "src")), P(("pairs", "tgt")), P("pairs", None)),
        check_vma=False,
    )
```

time: 312 us -> 48 us (0.15)
  blocking collectives: 185 us -> 0 us
  waiting for transfers between devices: 62.4 us -> 0 us
  Pallas kernels: 0 us -> 42.3 us
  matrix products: 21 us -> 0 us
  between operations: 14.2 us -> 0.65 us
  starting transfers between devices: 13.4 us -> 0 us
  other arithmetic: 12.7 us -> 0 us
    psum x2 -> x0, blocking collectives: 115 us -> none  [shards(): core_matrix = -2.0 * lax.psum(core_part, ('src', 'tgt'))]
    all_gather x7 -> x0, blocking collectives: 70 us -> none  [the longest x2 60.8 us: shards(): tgt_dual = lax.all_gather(dual_piece, 'src', axis=0, tiled=True)]
    all_gather x1 -> x0, waiting for transfers between devices: 42.7 us -> none  [shards(): tgt_rows = lax.all_gather(tgt_feat, 'src', axis=1, tiled=True)]
    pallas_call x0 -> x1, Pallas kernels: none -> 42.3 us  [shards(): pl.pallas_call(functools.partial(kernel, dims), out_shape=(jax.ShapeDtype...]
    dot_general x8 -> x0, matrix products: 21 us -> none  [the longest x2 12.4 us: shards(): weighted = jnp.dot(coupling, tgt_left, precision=HIGH)]
    all_to_all x4 -> x0, waiting for transfers between devices: 19 us -> none  [the longest x2 13.2 us: shards(): lax.all_to_all(col_total[None, :], 'src', split_axis=1, concat_axis=0, ti...]
    all_to_all x4 -> x0, starting transfers between devices: 13.4 us -> none  [the longest x2 6.71 us: shards(): lax.all_to_all(col_max[None, :], 'src', split_axis=1, concat_axis=0, tile...]
    reduce_sum x7 -> x0, other arithmetic: 9.53 us -> none  [the longest x2 7.45 us: shards(): col_total = jnp.sum(col_exp, axis=0)]
  transfers between devices with their start and end apart: 5 -> 0, of which waited for: 5 -> 0; matrix products, arithmetic and copies ran while one was open for 3% -> 0% of each run, Pallas kernels for 0% -> 0%
where the time goes in v1:
time: 48 us; the launch traced here: 47.7 us
  Pallas kernels  42.3 us (88%)
  local copies, waits for them, and re-layouts  4.81 us (10%)
  between operations  0.65 us (1%)
    pallas_call x1, Pallas kernels, shards(): pl.pallas_call(functools.partial(kernel, dims), out_shape=(jax.ShapeDtype...  42.3 us
    unnamed x11, local copies, waits for them, and re-layouts  4.81 us

profile of v1, /device:TPU:0, one launch (start us, length us, event | category | flops | bytes accessed | tf_op | source)
XLA Modules:
  0.0 47.7 jit_solution(1646827389616761031)
XLA Ops:
  0.6 0.0 copy-start
  0.6 0.9 %copy-done = f32[8192,4]{0,1:T(4,128)S(1)} copy-done((f32[8192,4]{0,1:T(4,128)S(1)}, f32[8192,4]{0,1:T(4,128)}, u32[]{:S(2)}) %copy-start) | copy-done | bytes 131096
  1.5 0.0 copy-start.1
  1.5 0.8 %copy-done.1 = f32[8192]{0:T(1024)S(1)} copy-done((f32[8192]{0:T(1024)S(1)}, f32[8192]{0:T(1024)}, u32[]{:S(2)}) %copy-start.1) | copy-done | bytes 32792
  2.3 0.0 copy-start.2
  2.3 0.7 %copy-done.2 = f32[34,34]{1,0:T(8,128)S(1)} copy-done((f32[34,34]{1,0:T(8,128)S(1)}, f32[34,34]{1,0:T(8,128)}, u32[]{:S(2)}) %copy-start.2) | copy-done | bytes 4648
  3.0 0.0 copy-start.3
  3.0 0.7 %copy-done.3 = f32[128,16]{0,1:T(8,128)S(1)} copy-done((f32[128,16]{0,1:T(8,128)S(1)}, f32[128,16]{0,1:T(8,128)}, u32[]{:S(2)}) %copy-start.3) | copy-done | bytes 8216
  3.7 42.3 %shard_map.67 = (f32[1,128]{1,0:T(1,128)S(1)}, f32[8,8,128]{2,1,0:T(8,128)S(1)}, f32[34,34]{1,0:T(8,128)S(1)}) custom-call(f32[16,128]{1,0:T(8,128)S(1)} %bitcast.12, f32[8,32,128]{2,1,0:T(8,128)S(1)} %bitcast.9, f32[8,8,128]{2,1,0:T(8,128)S(1)} %bitcast.11, f32[34,34]{1,0:T(8,128)S(1)} %copy-done.2), custom_call_target="tpu_custom_call" | custom-call | tf_op jit(solution)/shard_map/pallas_call | solution.py:276
  46.0 0.5 %copy.11 = f32[128]{0:T(128)} copy(f32[128]{0:T(128)S(1)} %bitcast.13) | data formatting | bytes 1024
  46.5 0.6 %copy.12 = f32[8192]{0:T(1024)} copy(f32[8192]{0:T(1024)S(1)} %bitcast.10) | data formatting | bytes 65536
  47.1 0.6 %copy.13 = f32[34,34]{1,0:T(8,128)} copy(f32[34,34]{1,0:T(8,128)S(1)} %get-tuple-element.14) | data formatting | bytes 9248
Async XLA Ops:
  0.6 0.9 %copy-start = (f32[8192,4]{0,1:T(4,128)S(1)}, f32[8192,4]{0,1:T(4,128)}, u32[]{:S(2)}) copy-start(f32[8192,4]{0,1:T(4,128)} %param.5) | copy-start | bytes 393220
  1.5 0.8 %copy-start.1 = (f32[8192]{0:T(1024)S(1)}, f32[8192]{0:T(1024)}, u32[]{:S(2)}) copy-start(f32[8192]{0:T(1024)} %param.6) | copy-start | bytes 98308
  2.3 0.7 %copy-start.2 = (f32[34,34]{1,0:T(8,128)S(1)}, f32[34,34]{1,0:T(8,128)}, u32[]{:S(2)}) copy-start(f32[34,34]{1,0:T(8,128)} %core_ref.1) | copy-start | bytes 13876
  3.0 0.7 %copy-start.3 = (f32[128,16]{0,1:T(8,128)S(1)}, f32[128,16]{0,1:T(8,128)}, u32[]{:S(2)}) copy-start(f32[128,16]{0,1:T(8,128)} %param.4) | copy-start | bytes 24580

commit v2 on v1

--- a/solution.py
+++ b/solution.py
@@ -35,8 +35,8 @@
 
 def kernel(
     dims, src_ref, tgt_ref, dual_ref, core_ref, u_out, g_out, core_out,
-    srcbuf, tgtbuf, lsebuf, corebuf, gbuf, sl, sr, tl, tr, sls, srs, tls, trt, sps, logits, gcol, weighted, urow, square,
-    send_sem, recv_sem,
+    srcbuf, tgtall, tgtbuf, dualbuf, corein, lsebuf, corebuf, gbuf, sl, sr, tl, tr, sls, srs, tls, trt, sps, logits, gcol, weighted, urow, square,
+    send_sem, recv_sem, local_sem,
 ):
     S, T, rows, cols, fs, ft, feat, ns, nt = dims
     D = S * T
@@ -44,78 +44,80 @@
     st = -(-rank // 8) * 8
     jr = cols // LANES
     nr = rows // LANES
+    last = 2 + 2 * OUTER
     s, t = lax.axis_index("src"), lax.axis_index("tgt")
     me = s * T + t
 
     def everyone(act):
         def body(k, unused):
-            peer = lax.rem(me + k, D)
-            act(peer, peer // T, lax.rem(peer, T))
+            ps = lax.rem(s + k, S)
+            for h in range(T):
+                pt = lax.rem(t + h, T)
+                act(ps, pt)
             return unused
 
-        lax.fori_loop(1, D, body, 0)
+        lax.fori_loop(1, S, body, 0, unroll=S <= 8)
+        for h in range(1, T):
+            act(s, lax.rem(t + h, T))
 
     def column(act):
         def body(k, unused):
             act(lax.rem(s + k, S))
             return unused
 
-        lax.fori_loop(1, S, body, 0)
-
-    def remote(phase, src, dst, out_id, in_id, device):
+        lax.fori_loop(1, S, body, 0, unroll=S <= 8)
+
+    def remote(phase, src, dst, device):
         return pltpu.make_async_remote_copy(
-            src_ref=src, dst_ref=dst, send_sem=send_sem.at[phase, out_id], recv_sem=recv_sem.at[phase, in_id],
+            src_ref=src, dst_ref=dst, send_sem=send_sem.at[phase], recv_sem=recv_sem.at[phase],
             device_id=device, device_id_type=MESH,
         )
 
-    def share(phase, buf, k):
-        def act(peer, ps, pt):
-            remote(phase, buf.at[k, me], buf.at[k, me], peer, me, {"src": ps, "tgt": pt}).start()
+    def share(phase, slots):
+        def act(ps, pt):
+            remote(phase, slots.at[me], slots.at[me], {"src": ps, "tgt": pt}).start()
 
         everyone(act)
 
-    def shared(phase, buf, k):
-        def act(peer, ps, pt):
-            remote(phase, buf.at[k, peer], buf.at[k, peer], peer, peer, {"src": ps, "tgt": pt}).wait_recv()
-
-        everyone(act)
-
-    def sent(phase, buf, k):
-        def act(peer, ps, pt):
-            remote(phase, buf.at[k, me], buf.at[k, me], peer, me, {"src": ps, "tgt": pt}).wait_send()
-
-        everyone(act)
-
+    def bytes_of(phase, slots, count):
+        part = slots.at[pl.ds(0, count - 1)]
+        return remote(phase, part, part, {"src": lax.rem(s + 1, S)})
+
+    copies = [
+        pltpu.make_async_copy(src_ref, srcbuf.at[me], local_sem.at[0]),
+        pltpu.make_async_copy(tgt_ref, tgtall, local_sem.at[1]),
+        pltpu.make_async_copy(dual_ref.at[s], dualbuf, local_sem.at[2]),
+        pltpu.make_async_copy(core_ref, corein, local_sem.at[3]),
+    ]
+    for copy in copies:
+        copy.start()
     barrier = pltpu.get_barrier_semaphore()
 
-    def greet(peer, ps, pt):
+    def greet(ps, pt):
         pl.semaphore_signal(barrier, inc=1, device_id={"src": ps, "tgt": pt}, device_id_type=MESH)
 
     everyone(greet)
-    srcbuf[s, t] = src_ref[...]
-    tgtbuf[s] = tgt_ref[s]
-    own_dual = dual_ref[s] * (1.0 / UNIT)
+    for copy in copies:
+        copy.wait()
+    tgtbuf[s] = tgtall[s]
+    own_dual = dualbuf[...] * (1.0 / UNIT)
     for r in range(jr):
         gcol[r * LANES : (r + 1) * LANES, :] = jnp.broadcast_to(own_dual[r : r + 1, :], (LANES, LANES)).T
     square[...] = jnp.zeros_like(square)
-    square[:rank, :rank] = core_ref[...]
+    square[:rank, :rank] = corein[...]
     turned = square[...].T[:st, :]
     pl.semaphore_wait(barrier, D - 1)
 
     def send_tgt(ps):
-        remote(1, tgt_ref.at[ps], tgtbuf.at[s], ps, s, {"src": ps}).start()
+        remote(1, tgtall.at[ps], tgtbuf.at[s], {"src": ps}).start()
 
     column(send_tgt)
 
-    def send_src(peer, ps, pt):
-        remote(0, src_ref, srcbuf.at[s, t], peer, me, {"src": ps, "tgt": pt}).start()
+    def send_src(ps, pt):
+        remote(0, srcbuf.at[me], srcbuf.at[me], {"src": ps, "tgt": pt}).start()
 
     everyone(send_src)
-
-    def get_tgt(ps):
-        remote(1, tgt_ref.at[ps], tgtbuf.at[ps], ps, ps, {"src": ps}).wait_recv()
-
-    column(get_tgt)
+    bytes_of(1, tgtbuf, S).wait_recv()
 
     def lift(left, right):
         values = right[2:rank, :]
@@ -144,13 +146,10 @@
     trt[...] = stacked((t0, t1, t0, t1, t2, t0), deep).T.astype(BF16)
     tls[...] = stacked(split3(tl[...]), wide).astype(BF16)
 
-    def get_src(peer, ps, pt):
-        remote(0, src_ref, srcbuf.at[ps, pt], peer, peer, {"src": ps, "tgt": pt}).wait_recv()
-
-    everyone(get_src)
+    bytes_of(0, srcbuf, D).wait_recv()
     for k in range(S):
         for h in range(T):
-            sr[2 + h * fs : 2 + (h + 1) * fs, k * rows : (k + 1) * rows] = srcbuf[k, h]
+            sr[2 + h * fs : 2 + (h + 1) * fs, k * rows : (k + 1) * rows] = srcbuf[k * T + h]
     lift(sl, sr)
     sls[...] = stacked(split3(sl[...]), wide).astype(BF16)
     srs[...] = stacked(split3(sr[...]), wide).T.astype(BF16)
@@ -176,8 +175,8 @@
                 top = jnp.max(here, axis=0, keepdims=True)
                 total = jnp.sum(jnp.exp2(here - top), axis=0, keepdims=True)
                 lsebuf[step, me, at : at + 1, :] = top + jnp.log2(total)
-        share(2 + 2 * step, lsebuf, step)
-        shared(2 + 2 * step, lsebuf, step)
+        share(2 + 2 * step, lsebuf.at[step])
+        bytes_of(2 + 2 * step, lsebuf.at[step], D).wait_recv()
         top = jnp.max(lsebuf[step], axis=0)
         total = jnp.sum(jnp.exp2(lsebuf[step] - top[None]), axis=0)
         urow[...] = -math.log2(ns) - (top + jnp.log2(total))
@@ -201,7 +200,7 @@
                 gbuf[s, r : r + 1, :] = gcol[r * LANES : (r + 1) * LANES, :].T[0:1, :] * UNIT
 
             def send_g(ps):
-                remote(1 + 2 * OUTER + 1, gbuf.at[s], gbuf.at[s], ps, s, {"src": ps}).start()
+                remote(last, gbuf.at[s], gbuf.at[s], {"src": ps}).start()
 
             column(send_g)
         ext = jnp.dot(tls[...], weighted[...], preferred_element_type=F32)
@@ -217,8 +216,8 @@
                     piece = shifted(kt[n * 8 : n * 8 + 8, :], k * st)
                     tile = piece if tile is None else tile + piece
             corebuf[step, me, group * 8 : group * 8 + 8, :] = tile
-        share(3 + 2 * step, corebuf, step)
-        shared(3 + 2 * step, corebuf, step)
+        share(3 + 2 * step, corebuf.at[step])
+        bytes_of(3 + 2 * step, corebuf.at[step], D).wait_recv()
         summed = -2.0 * jnp.sum(corebuf[step], axis=0)
         turned = jnp.concatenate(
             [
@@ -231,25 +230,23 @@
     square[:st, :] = turned
     core_out[...] = square[...].T[:rank, :rank]
 
-    def get_g(ps):
-        remote(1 + 2 * OUTER + 1, gbuf.at[ps], gbuf.at[ps], ps, ps, {"src": ps}).wait_recv()
-
-    column(get_g)
+    bytes_of(last, gbuf, S).wait_recv()
     g_out[...] = gbuf[...]
-
-    def done_tgt(ps):
-        remote(1, tgt_ref.at[ps], tgtbuf.at[s], ps, s, {"src": ps}).wait_send()
-        remote(1 + 2 * OUTER + 1, gbuf.at[s], gbuf.at[s], ps, s, {"src": ps}).wait_send()
-
-    column(done_tgt)
-
-    def done_src(peer, ps, pt):
-        remote(0, src_ref, srcbuf.at[s, t], peer, me, {"src": ps, "tgt": pt}).wait_send()
-
-    everyone(done_src)
+    bytes_of(0, srcbuf, D).wait_send()
+    bytes_of(1, tgtbuf, S).wait_send()
+    bytes_of(last, gbuf, S).wait_send()
     for step in range(OUTER):
-        sent(2 + 2 * step, lsebuf, step)
-        sent(3 + 2 * step, corebuf, step)
+        bytes_of(2 + 2 * step, lsebuf.at[step], D).wait_send()
+        bytes_of(3 + 2 * step, corebuf.at[step], D).wait_send()
+
+
+def place(*refs):
+    count = (len(refs) - 1) // 2
+    copies = [pltpu.make_async_copy(refs[k], refs[count + k], refs[-1].at[k]) for k in range(count)]
+    for copy in copies:
+        copy.start()
+    for copy in copies:
+        copy.wait()
 
 
 def shards(src_feat, tgt_feat, tgt_dual, core_matrix):
@@ -280,11 +277,14 @@
             jax.ShapeDtypeStruct((S, jr, LANES), F32),
             jax.ShapeDtypeStruct((rank, rank), F32),
         ),
-        in_specs=[vmem] * 4,
+        in_specs=[pl.BlockSpec(memory_space=pltpu.HBM)] * 4,
         out_specs=(vmem,) * 3,
         scratch_shapes=[
-            pltpu.VMEM((S, T, fs, rows), F32),
+            pltpu.VMEM((D, fs, rows), F32),
             pltpu.VMEM((S, jr * ft, LANES), F32),
+            pltpu.VMEM((S, jr * ft, LANES), F32),
+            pltpu.VMEM((jr, LANES), F32),
+            pltpu.VMEM((rank, rank), F32),
             pltpu.VMEM((OUTER, D, ns // LANES, LANES), F32),
             pltpu.VMEM((OUTER, D, groups * 8, LANES), F32),
             pltpu.VMEM((S, jr, LANES), F32),
@@ -302,13 +302,23 @@
             pltpu.VMEM((cols, 2 * wide), BF16),
             pltpu.VMEM((ns // LANES, LANES), F32),
             pltpu.VMEM((LANES, LANES), F32),
-            pltpu.SemaphoreType.DMA((phases, D)),
-            pltpu.SemaphoreType.DMA((phases, D)),
+            pltpu.SemaphoreType.DMA((phases,)),
+            pltpu.SemaphoreType.DMA((phases,)),
+            pltpu.SemaphoreType.DMA((4,)),
         ],
         compiler_params=pltpu.CompilerParams(
-            collective_id=0, has_side_effects=True, vmem_limit_bytes=48 * 1024 * 1024
+            collective_id=0, has_side_effects=True, vmem_limit_bytes=64 * 1024 * 1024
         ),
     )(src, tgt, dual, core_matrix)
+    placed = [u, g, core]
+    u, g, core = pl.pallas_call(
+        place,
+        out_shape=[jax.ShapeDtypeStruct(x.shape, x.dtype) for x in placed],
+        in_specs=[pl.BlockSpec(memory_space=pltpu.HBM)] * 3,
+        out_specs=[pl.BlockSpec(memory_space=pltpu.HBM)] * 3,
+        scratch_shapes=[pltpu.SemaphoreType.DMA((3,))],
+        compiler_params=pltpu.CompilerParams(vmem_limit_bytes=64 * 1024 * 1024),
+    )(*placed)
     return u.reshape(rows), g.reshape(held), core
 
 

time: 48 us -> 43.6 us (0.908)
  local copies, waits for them, and re-layouts: 4.81 us -> 0 us
  Pallas kernels: 42.3 us -> 42.8 us
    unnamed x11 -> x0, local copies, waits for them, and re-layouts: 4.81 us -> none
    pallas_call x0 -> x1, Pallas kernels: none -> 2.67 us  [shards(): pl.pallas_call(place, out_shape=[jax.ShapeDtypeStruct(x.shape, x.dtype) f...]
    pallas_call x1, Pallas kernels: 42.3 us -> 40.1 us  [shards(): pl.pallas_call(functools.partial(kernel, dims), out_shape=(jax.ShapeDtype...]
where the time goes in v2:
time: 43.6 us; the launch traced here: 43.4 us
  Pallas kernels  42.8 us (98%)
  between operations  0.64 us (1%)
    pallas_call x1, Pallas kernels, shards(): pl.pallas_call(functools.partial(kernel, dims), out_shape=(jax.ShapeDtype...  40.1 us
    pallas_call x1, Pallas kernels, shards(): pl.pallas_call(place, out_shape=[jax.ShapeDtypeStruct(x.shape, x.dtype) f...  2.67 us

profile of v2, /device:TPU:0, one launch (start us, length us, event | category | flops | bytes accessed | tf_op | source)
XLA Modules:
  0.0 43.4 jit_solution(984751763805179576)
XLA Ops:
  0.6 40.1 %shard_map.67 = (f32[1,128]{1,0:T(1,128)}, f32[8,8,128]{2,1,0:T(8,128)}, f32[34,34]{1,0:T(8,128)}) custom-call(f32[16,128]{1,0:T(8,128)} %bitcast.11, f32[8,32,128]{2,1,0:T(8,128)} %bitcast.9, f32[8,8,128]{2,1,0:T(8,128)} %bitcast.10, f32[34,34]{1,0:T(8,128)} %core_ref.1), custom_call_target="tpu_custom_call" | custom-call | tf_op jit(solution)/shard_map/pallas_call | solution.py:273
  40.7 2.7 %shard_map.68 = (f32[1,128]{1,0:T(1,128)}, f32[8,8,128]{2,1,0:T(8,128)}, f32[34,34]{1,0:T(8,128)}) custom-call(f32[1,128]{1,0:T(1,128)} %get-tuple-element.9.refs_0_, f32[8,8,128]{2,1,0:T(8,128)} %get-tuple-element.10.refs_1_, f32[34,34]{1,0:T(8,128)} %get-tuple-element.11.refs_2_), custom_call_target="tpu_custom_call" | custom-call | tf_op jit(solution)/shard_map/pallas_call | solution.py:314

commit v3 on v2

--- a/solution.py
+++ b/solution.py
@@ -35,7 +35,7 @@
 
 def kernel(
     dims, src_ref, tgt_ref, dual_ref, core_ref, u_out, g_out, core_out,
-    srcbuf, tgtall, tgtbuf, dualbuf, corein, lsebuf, corebuf, gbuf, sl, sr, tl, tr, sls, srs, tls, trt, sps, logits, gcol, weighted, urow, square,
+    srcbuf, tgtall, tgtbuf, dualbuf, corein, lsebuf, corebuf, gbuf, sl, sr, tl, tr, sls, srs, tls, trt, sps, logits, gcol, weighted, ehigh, elow, urow, square,
     send_sem, recv_sem, local_sem,
 ):
     S, T, rows, cols, fs, ft, feat, ns, nt = dims
@@ -119,17 +119,13 @@
     everyone(send_src)
     bytes_of(1, tgtbuf, S).wait_recv()
 
-    def lift(left, right):
-        values = right[2:rank, :]
+    def lift(ref, values, ahead, scale):
+        ref[rank:, :] = jnp.zeros_like(ref[rank:, :])
         squares = jnp.sum(values * values, axis=0, keepdims=True)
         ones = jnp.ones_like(squares)
-        left[rank:, :] = jnp.zeros_like(left[rank:, :])
-        right[rank:, :] = jnp.zeros_like(right[rank:, :])
-        left[0:1, :] = squares
-        left[1:2, :] = ones
-        left[2:rank, :] = -2.0 * values
-        right[0:1, :] = ones
-        right[1:2, :] = squares
+        ref[0:1, :] = squares if ahead else ones
+        ref[1:2, :] = ones if ahead else squares
+        ref[2:rank, :] = values if scale is None else scale * values
 
     def stacked(parts, height):
         width = parts[0].shape[1]
@@ -141,18 +137,16 @@
     for k in range(S):
         for r in range(jr):
             tr[2 + k * ft : 2 + (k + 1) * ft, r * LANES : (r + 1) * LANES] = tgtbuf[k, r * ft : (r + 1) * ft, :]
-    lift(tl, tr)
+    lift(tr, tr[2:rank, :], False, None)
     t0, t1, t2 = split3(tr[...])
-    trt[...] = stacked((t0, t1, t0, t1, t2, t0), deep).T.astype(BF16)
-    tls[...] = stacked(split3(tl[...]), wide).astype(BF16)
+    trt[...] = stacked((t0, t1, t0, t1, t2, t0), deep).astype(BF16).T
 
     bytes_of(0, srcbuf, D).wait_recv()
     for k in range(S):
         for h in range(T):
             sr[2 + h * fs : 2 + (h + 1) * fs, k * rows : (k + 1) * rows] = srcbuf[k * T + h]
-    lift(sl, sr)
+    lift(sl, sr[2:rank, :], True, -2.0)
     sls[...] = stacked(split3(sl[...]), wide).astype(BF16)
-    srs[...] = stacked(split3(sr[...]), wide).T.astype(BF16)
 
     per = LANES // st
     block = min(256, ns)
@@ -170,12 +164,23 @@
             part = jnp.dot(trt[...], sps[:, b * block : (b + 1) * block], preferred_element_type=F32)
             for h in range(block // LANES):
                 at = b * block // LANES + h
-                here = part[:, h * LANES : (h + 1) * LANES] + gcol[...]
-                logits[:, at * LANES : (at + 1) * LANES] = here
-                top = jnp.max(here, axis=0, keepdims=True)
-                total = jnp.sum(jnp.exp2(here - top), axis=0, keepdims=True)
+                tops, totals = [], []
+                for c in range(cols // chunk):
+                    rows_c = slice(c * chunk, (c + 1) * chunk)
+                    here = part[rows_c, h * LANES : (h + 1) * LANES] + gcol[rows_c, :]
+                    logits[rows_c, at * LANES : (at + 1) * LANES] = here
+                    top = jnp.max(here, axis=0, keepdims=True)
+                    tops.append(top)
+                    totals.append(jnp.sum(jnp.exp2(here - top), axis=0, keepdims=True))
+                top = functools.reduce(jnp.maximum, tops)
+                total = sum(x * jnp.exp2(y - top) for x, y in zip(totals, tops))
                 lsebuf[step, me, at : at + 1, :] = top + jnp.log2(total)
         share(2 + 2 * step, lsebuf.at[step])
+        if step == 0:
+            lift(tl, tr[2:rank, :], True, -2.0)
+            tls[...] = stacked(split3(tl[...]), wide).astype(BF16)
+            lift(sr, sr[2:rank, :], False, None)
+            srs[...] = stacked(split3(sr[...]), wide).astype(BF16).T
         bytes_of(2 + 2 * step, lsebuf.at[step], D).wait_recv()
         top = jnp.max(lsebuf[step], axis=0)
         total = jnp.sum(jnp.exp2(lsebuf[step] - top[None]), axis=0)
@@ -183,26 +188,23 @@
         u_all = jnp.concatenate([urow[k : k + 1, :] for k in range(ns // LANES)], axis=1)
         for c in range(cols // chunk):
             sl_c = slice(c * chunk, (c + 1) * chunk)
-            x = logits[sl_c, :] + u_all
-            top = jnp.max(x, axis=1, keepdims=True)
-            e = jnp.exp2(x - top)
-            high = e.astype(BF16)
-            low = (e - high.astype(F32)).astype(BF16)
-            acc = jnp.dot(high, srs[...], preferred_element_type=F32) + jnp.dot(low, srs[...], preferred_element_type=F32)
+            tops = []
+            for k in range(chunk // 16):
+                x = logits[c * chunk + k * 16 : c * chunk + (k + 1) * 16, :] + u_all
+                top = jnp.max(x, axis=1, keepdims=True)
+                e = jnp.exp2(x - top)
+                high = e.astype(BF16)
+                ehigh[c, k * 16 : (k + 1) * 16, :] = high
+                elow[c, k * 16 : (k + 1) * 16, :] = (e - high.astype(F32)).astype(BF16)
+                tops.append(top)
+            top = jnp.concatenate(tops, axis=0)
+            acc = jnp.dot(ehigh[c], srs[...], preferred_element_type=F32) + jnp.dot(elow[c], srs[...], preferred_element_type=F32)
             total = acc[:, 0:1]
             scaled = acc * (1.0 / total)
             first = scaled.astype(BF16)
             weighted[sl_c, :wide] = first
             weighted[sl_c, wide:] = (scaled - first.astype(F32)).astype(BF16)
             gcol[sl_c, :] = (gcol[sl_c, :] - math.log2(nt)) - (top + jnp.log2(total))
-        if step == OUTER - 1:
-            for r in range(jr):
-                gbuf[s, r : r + 1, :] = gcol[r * LANES : (r + 1) * LANES, :].T[0:1, :] * UNIT
-
-            def send_g(ps):
-                remote(last, gbuf.at[s], gbuf.at[s], {"src": ps}).start()
-
-            column(send_g)
         ext = jnp.dot(tls[...], weighted[...], preferred_element_type=F32)
         ext = ext[:, :wide] + ext[:, wide:]
         kt = ext[:st] + (ext[st : 2 * st] + ext[2 * st : 3 * st])
@@ -217,6 +219,14 @@
                     tile = piece if tile is None else tile + piece
             corebuf[step, me, group * 8 : group * 8 + 8, :] = tile
         share(3 + 2 * step, corebuf.at[step])
+        if step == OUTER - 1:
+            for r in range(jr):
+                gbuf[s, r : r + 1, :] = gcol[r * LANES : (r + 1) * LANES, :].T[0:1, :] * UNIT
+
+            def send_g(ps):
+                remote(last, gbuf.at[s], gbuf.at[s], {"src": ps}).start()
+
+            column(send_g)
         bytes_of(3 + 2 * step, corebuf.at[step], D).wait_recv()
         summed = -2.0 * jnp.sum(corebuf[step], axis=0)
         turned = jnp.concatenate(
@@ -238,15 +248,6 @@
     for step in range(OUTER):
         bytes_of(2 + 2 * step, lsebuf.at[step], D).wait_send()
         bytes_of(3 + 2 * step, corebuf.at[step], D).wait_send()
-
-
-def place(*refs):
-    count = (len(refs) - 1) // 2
-    copies = [pltpu.make_async_copy(refs[k], refs[count + k], refs[-1].at[k]) for k in range(count)]
-    for copy in copies:
-        copy.start()
-    for copy in copies:
-        copy.wait()
 
 
 def shards(src_feat, tgt_feat, tgt_dual, core_matrix):
@@ -265,6 +266,7 @@
     deep = -(-6 * st // LANES) * LANES
     wide = -(-3 * st // LANES) * LANES
     dims = (S, T, rows, cols, fs, ft, feat, ns, nt)
+    chunk = min(256, cols)
     src = src_feat.T
     tgt = tgt_feat.reshape(S * jr, LANES, ft).transpose(0, 2, 1).reshape(S, jr * ft, LANES)
     dual = tgt_dual.reshape(S, jr, LANES)
@@ -300,6 +302,8 @@
             pltpu.VMEM((cols, ns), F32),
             pltpu.VMEM((cols, LANES), F32),
             pltpu.VMEM((cols, 2 * wide), BF16),
+            pltpu.VMEM((cols // chunk, chunk, ns), BF16),
+            pltpu.VMEM((cols // chunk, chunk, ns), BF16),
             pltpu.VMEM((ns // LANES, LANES), F32),
             pltpu.VMEM((LANES, LANES), F32),
             pltpu.SemaphoreType.DMA((phases,)),
@@ -310,15 +314,6 @@
             collective_id=0, has_side_effects=True, vmem_limit_bytes=64 * 1024 * 1024
         ),
     )(src, tgt, dual, core_matrix)
-    placed = [u, g, core]
-    u, g, core = pl.pallas_call(
-        place,
-        out_shape=[jax.ShapeDtypeStruct(x.shape, x.dtype) for x in placed],
-        in_specs=[pl.BlockSpec(memory_space=pltpu.HBM)] * 3,
-        out_specs=[pl.BlockSpec(memory_space=pltpu.HBM)] * 3,
-        scratch_shapes=[pltpu.SemaphoreType.DMA((3,))],
-        compiler_params=pltpu.CompilerParams(vmem_limit_bytes=64 * 1024 * 1024),
-    )(*placed)
     return u.reshape(rows), g.reshape(held), core
 
 

time: 43.6 us -> 44.9 us (1.030)
  local copies, waits for them, and re-layouts: 0 us -> 3.18 us
  Pallas kernels: 42.8 us -> 40.8 us
    unnamed x0 -> x7, local copies, waits for them, and re-layouts: none -> 3.18 us
    pallas_call x1 -> x0, Pallas kernels: 2.67 us -> none  [shards(): pl.pallas_call(place, out_shape=[jax.ShapeDtypeStruct(x.shape, x.dtype) f...]
    pallas_call x1, Pallas kernels: 40.1 us -> 40.8 us  [shards(): pl.pallas_call(functools.partial(kernel, dims), out_shape=(jax.ShapeDtype...]
where the time goes in v3:
time: 44.9 us; the launch traced here: 44.7 us
  Pallas kernels  40.8 us (91%)
  local copies, waits for them, and re-layouts  3.18 us (7%)
  between operations  0.65 us (1%)
    pallas_call x1, Pallas kernels, shards(): pl.pallas_call(functools.partial(kernel, dims), out_shape=(jax.ShapeDtype...  40.8 us
    unnamed x7, local copies, waits for them, and re-layouts  3.18 us

profile of v3, /device:TPU:0, one launch (start us, length us, event | category | flops | bytes accessed | tf_op | source)
XLA Modules:
  0.0 44.7 jit_solution(132240735245571424)
XLA Ops:
  0.6 40.8 %shard_map.67 = (f32[1,128]{1,0:T(1,128)}, f32[8,8,128]{2,1,0:T(8,128)}, f32[34,34]{1,0:T(8,128)}) custom-call(f32[16,128]{1,0:T(8,128)} %bitcast.12, f32[8,32,128]{2,1,0:T(8,128)} %bitcast.9, f32[8,8,128]{2,1,0:T(8,128)} %bitcast.11, f32[34,34]{1,0:T(8,128)} %core_ref.1), custom_call_target="tpu_custom_call" | custom-call | tf_op jit(solution)/shard_map/pallas_call | solution.py:275
  41.5 0.0 copy-start.1
  41.5 0.7 %copy-done.1 = f32[1,128]{1,0:T(1,128)S(1)} copy-done((f32[1,128]{1,0:T(1,128)S(1)}, f32[1,128]{1,0:T(1,128)}, u32[]{:S(2)}) %copy-start.1) | copy-done | bytes 536
  42.2 0.5 %copy.11 = f32[128]{0:T(128)} copy(f32[128]{0:T(128)S(1)} %bitcast.13) | data formatting | bytes 1024
  42.7 0.0 copy-start
  42.7 1.4 %copy.12 = f32[8192]{0:T(1024)} copy(f32[8192]{0:T(1024)} %bitcast.10) | data formatting | bytes 65536
  44.1 0.0 copy-done
  44.1 0.6 %copy.13 = f32[34,34]{1,0:T(8,128)} copy(f32[34,34]{1,0:T(8,128)S(1)} %copy-done) | data formatting | bytes 9248
Async XLA Ops:
  41.5 0.7 %copy-start.1 = (f32[1,128]{1,0:T(1,128)S(1)}, f32[1,128]{1,0:T(1,128)}, u32[]{:S(2)}) copy-start(f32[1,128]{1,0:T(1,128)} %get-tuple-element.6) | copy-start | bytes 1540
  42.7 1.4 %copy-start = (f32[34,34]{1,0:T(8,128)S(1)}, f32[34,34]{1,0:T(8,128)}, u32[]{:S(2)}) copy-start(f32[34,34]{1,0:T(8,128)} %get-tuple-element.14) | copy-start | bytes 13876

commit v4 on v3

--- a/solution.py
+++ b/solution.py
@@ -25,6 +25,11 @@
     return high, mid, rest - mid
 
 
+def joined(logs):
+    top = jnp.max(logs, axis=0)
+    return top + jnp.log2(jnp.sum(jnp.exp2(logs - top[None]), axis=0))
+
+
 def lanes_below(x, count):
     return jnp.where(lax.broadcasted_iota(jnp.int32, x.shape, 1) < count, x, 0.0)
 
@@ -35,30 +40,20 @@
 
 def kernel(
     dims, src_ref, tgt_ref, dual_ref, core_ref, u_out, g_out, core_out,
-    srcbuf, tgtall, tgtbuf, dualbuf, corein, lsebuf, corebuf, gbuf, sl, sr, tl, tr, sls, srs, tls, trt, sps, logits, gcol, weighted, ehigh, elow, urow, square,
+    srcbuf, tgtall, tgtbuf, dualbuf, corein, lsepair, lsebuf, corepair, corebuf, gbuf, sl, sr, tl, tr, sls, srs, tls, trt, sps, logits, gcol, weighted, ehigh, elow, urow, square,
     send_sem, recv_sem, local_sem,
 ):
     S, T, rows, cols, fs, ft, feat, ns, nt = dims
-    D = S * T
     rank = feat + 2
     st = -(-rank // 8) * 8
     jr = cols // LANES
     nr = rows // LANES
-    last = 2 + 2 * OUTER
+    last = 3 + 4 * OUTER
     s, t = lax.axis_index("src"), lax.axis_index("tgt")
-    me = s * T + t
-
-    def everyone(act):
-        def body(k, unused):
-            ps = lax.rem(s + k, S)
-            for h in range(T):
-                pt = lax.rem(t + h, T)
-                act(ps, pt)
-            return unused
-
-        lax.fori_loop(1, S, body, 0, unroll=S <= 8)
+
+    def beside(act):
         for h in range(1, T):
-            act(s, lax.rem(t + h, T))
+            act(lax.rem(t + h, T))
 
     def column(act):
         def body(k, unused):
@@ -73,18 +68,18 @@
             device_id=device, device_id_type=MESH,
         )
 
-    def share(phase, slots):
-        def act(ps, pt):
-            remote(phase, slots.at[me], slots.at[me], {"src": ps, "tgt": pt}).start()
-
-        everyone(act)
-
     def bytes_of(phase, slots, count):
         part = slots.at[pl.ds(0, count - 1)]
         return remote(phase, part, part, {"src": lax.rem(s + 1, S)})
 
+    def over_tgt(phase, slots):
+        beside(lambda pt: remote(phase, slots.at[t], slots.at[t], {"tgt": pt}).start())
+
+    def over_src(phase, slots):
+        column(lambda ps: remote(phase, slots.at[s], slots.at[s], {"src": ps}).start())
+
     copies = [
-        pltpu.make_async_copy(src_ref, srcbuf.at[me], local_sem.at[0]),
+        pltpu.make_async_copy(src_ref, srcbuf.at[t, s], local_sem.at[0]),
         pltpu.make_async_copy(tgt_ref, tgtall, local_sem.at[1]),
         pltpu.make_async_copy(dual_ref.at[s], dualbuf, local_sem.at[2]),
         pltpu.make_async_copy(core_ref, corein, local_sem.at[3]),
@@ -93,10 +88,11 @@
         copy.start()
     barrier = pltpu.get_barrier_semaphore()
 
-    def greet(ps, pt):
-        pl.semaphore_signal(barrier, inc=1, device_id={"src": ps, "tgt": pt}, device_id_type=MESH)
-
-    everyone(greet)
+    def greet(device):
+        pl.semaphore_signal(barrier, inc=1, device_id=device, device_id_type=MESH)
+
+    column(lambda ps: greet({"src": ps}))
+    beside(lambda pt: greet({"tgt": pt}))
     for copy in copies:
         copy.wait()
     tgtbuf[s] = tgtall[s]
@@ -106,17 +102,12 @@
     square[...] = jnp.zeros_like(square)
     square[:rank, :rank] = corein[...]
     turned = square[...].T[:st, :]
-    pl.semaphore_wait(barrier, D - 1)
-
-    def send_tgt(ps):
-        remote(1, tgtall.at[ps], tgtbuf.at[s], {"src": ps}).start()
-
-    column(send_tgt)
-
-    def send_src(ps, pt):
-        remote(0, srcbuf.at[me], srcbuf.at[me], {"src": ps, "tgt": pt}).start()
-
-    everyone(send_src)
+    pl.semaphore_wait(barrier, S + T - 2)
+
+    over_src(0, srcbuf.at[t])
+    column(lambda ps: remote(1, tgtall.at[ps], tgtbuf.at[s], {"src": ps}).start())
+    bytes_of(0, srcbuf.at[t], S).wait_recv()
+    over_tgt(2, srcbuf)
     bytes_of(1, tgtbuf, S).wait_recv()
 
     def lift(ref, values, ahead, scale):
@@ -141,10 +132,10 @@
     t0, t1, t2 = split3(tr[...])
     trt[...] = stacked((t0, t1, t0, t1, t2, t0), deep).astype(BF16).T
 
-    bytes_of(0, srcbuf, D).wait_recv()
+    bytes_of(2, srcbuf, T).wait_recv()
     for k in range(S):
         for h in range(T):
-            sr[2 + h * fs : 2 + (h + 1) * fs, k * rows : (k + 1) * rows] = srcbuf[k * T + h]
+            sr[2 + h * fs : 2 + (h + 1) * fs, k * rows : (k + 1) * rows] = srcbuf[h, k]
     lift(sl, sr[2:rank, :], True, -2.0)
     sls[...] = stacked(split3(sl[...]), wide).astype(BF16)
 
@@ -174,17 +165,19 @@
                     totals.append(jnp.sum(jnp.exp2(here - top), axis=0, keepdims=True))
                 top = functools.reduce(jnp.maximum, tops)
                 total = sum(x * jnp.exp2(y - top) for x, y in zip(totals, tops))
-                lsebuf[step, me, at : at + 1, :] = top + jnp.log2(total)
-        share(2 + 2 * step, lsebuf.at[step])
+                lsepair[step, t, at : at + 1, :] = top + jnp.log2(total)
+        phase = 3 + 4 * step
+        over_tgt(phase, lsepair.at[step])
+        bytes_of(phase, lsepair.at[step], T).wait_recv()
+        lsebuf[step, s] = joined(lsepair[step])
+        over_src(phase + 1, lsebuf.at[step])
         if step == 0:
             lift(tl, tr[2:rank, :], True, -2.0)
             tls[...] = stacked(split3(tl[...]), wide).astype(BF16)
             lift(sr, sr[2:rank, :], False, None)
             srs[...] = stacked(split3(sr[...]), wide).astype(BF16).T
-        bytes_of(2 + 2 * step, lsebuf.at[step], D).wait_recv()
-        top = jnp.max(lsebuf[step], axis=0)
-        total = jnp.sum(jnp.exp2(lsebuf[step] - top[None]), axis=0)
-        urow[...] = -math.log2(ns) - (top + jnp.log2(total))
+        bytes_of(phase + 1, lsebuf.at[step], S).wait_recv()
+        urow[...] = -math.log2(ns) - joined(lsebuf[step])
         u_all = jnp.concatenate([urow[k : k + 1, :] for k in range(ns // LANES)], axis=1)
         for c in range(cols // chunk):
             sl_c = slice(c * chunk, (c + 1) * chunk)
@@ -217,17 +210,16 @@
                 if n * 8 < st:
                     piece = shifted(kt[n * 8 : n * 8 + 8, :], k * st)
                     tile = piece if tile is None else tile + piece
-            corebuf[step, me, group * 8 : group * 8 + 8, :] = tile
-        share(3 + 2 * step, corebuf.at[step])
+            corepair[step, t, group * 8 : group * 8 + 8, :] = tile
+        over_tgt(phase + 2, corepair.at[step])
+        bytes_of(phase + 2, corepair.at[step], T).wait_recv()
+        corebuf[step, s] = jnp.sum(corepair[step], axis=0)
+        over_src(phase + 3, corebuf.at[step])
         if step == OUTER - 1:
             for r in range(jr):
                 gbuf[s, r : r + 1, :] = gcol[r * LANES : (r + 1) * LANES, :].T[0:1, :] * UNIT
-
-            def send_g(ps):
-                remote(last, gbuf.at[s], gbuf.at[s], {"src": ps}).start()
-
-            column(send_g)
-        bytes_of(3 + 2 * step, corebuf.at[step], D).wait_recv()
+            over_src(last, gbuf)
+        bytes_of(phase + 3, corebuf.at[step], S).wait_recv()
         summed = -2.0 * jnp.sum(corebuf[step], axis=0)
         turned = jnp.concatenate(
             [
@@ -242,17 +234,26 @@
 
     bytes_of(last, gbuf, S).wait_recv()
     g_out[...] = gbuf[...]
-    bytes_of(0, srcbuf, D).wait_send()
+    bytes_of(0, srcbuf.at[t], S).wait_send()
     bytes_of(1, tgtbuf, S).wait_send()
+    bytes_of(2, srcbuf, T).wait_send()
+    for step in range(OUTER):
+        phase = 3 + 4 * step
+        bytes_of(phase, lsepair.at[step], T).wait_send()
+        bytes_of(phase + 1, lsebuf.at[step], S).wait_send()
+        bytes_of(phase + 2, corepair.at[step], T).wait_send()
+        bytes_of(phase + 3, corebuf.at[step], S).wait_send()
     bytes_of(last, gbuf, S).wait_send()
-    for step in range(OUTER):
-        bytes_of(2 + 2 * step, lsebuf.at[step], D).wait_send()
-        bytes_of(3 + 2 * step, corebuf.at[step], D).wait_send()
+
+
+def place(*refs):
+    count = len(refs) // 2
+    for k in range(count):
+        refs[count + k][...] = refs[k][...]
 
 
 def shards(src_feat, tgt_feat, tgt_dual, core_matrix):
     S, T = lax.axis_size("src"), lax.axis_size("tgt")
-    D = S * T
     rows, fs = src_feat.shape
     held, ft = tgt_feat.shape
     feat = fs * T
@@ -270,7 +271,7 @@
     src = src_feat.T
     tgt = tgt_feat.reshape(S * jr, LANES, ft).transpose(0, 2, 1).reshape(S, jr * ft, LANES)
     dual = tgt_dual.reshape(S, jr, LANES)
-    phases = 2 + 2 * OUTER + 1
+    phases = 4 + 4 * OUTER
     vmem = pl.BlockSpec(memory_space=pltpu.VMEM)
     u, g, core = pl.pallas_call(
         functools.partial(kernel, dims),
@@ -282,13 +283,15 @@
         in_specs=[pl.BlockSpec(memory_space=pltpu.HBM)] * 4,
         out_specs=(vmem,) * 3,
         scratch_shapes=[
-            pltpu.VMEM((D, fs, rows), F32),
+            pltpu.VMEM((T, S, fs, rows), F32),
             pltpu.VMEM((S, jr * ft, LANES), F32),
             pltpu.VMEM((S, jr * ft, LANES), F32),
             pltpu.VMEM((jr, LANES), F32),
             pltpu.VMEM((rank, rank), F32),
-            pltpu.VMEM((OUTER, D, ns // LANES, LANES), F32),
-            pltpu.VMEM((OUTER, D, groups * 8, LANES), F32),
+            pltpu.VMEM((OUTER, T, ns // LANES, LANES), F32),
+            pltpu.VMEM((OUTER, S, ns // LANES, LANES), F32),
+            pltpu.VMEM((OUTER, T, groups * 8, LANES), F32),
+            pltpu.VMEM((OUTER, S, groups * 8, LANES), F32),
             pltpu.VMEM((S, jr, LANES), F32),
             pltpu.VMEM((st, ns), F32),
             pltpu.VMEM((st, ns), F32),
@@ -314,6 +317,14 @@
             collective_id=0, has_side_effects=True, vmem_limit_bytes=64 * 1024 * 1024
         ),
     )(src, tgt, dual, core_matrix)
+    placed = [u, g, core]
+    u, g, core = pl.pallas_call(
+        place,
+        out_shape=[jax.ShapeDtypeStruct(x.shape, x.dtype) for x in placed],
+        in_specs=[vmem] * 3,
+        out_specs=[vmem] * 3,
+        compiler_params=pltpu.CompilerParams(vmem_limit_bytes=64 * 1024 * 1024),
+    )(*placed)
     return u.reshape(rows), g.reshape(held), core
 
 

time: 44.9 us -> 41.8 us (0.931)
  local copies, waits for them, and re-layouts: 3.18 us -> 0 us
    unnamed x7 -> x0, local copies, waits for them, and re-layouts: 3.18 us -> none
    pallas_call x0 -> x1, Pallas kernels: none -> 1.39 us  [shards(): pl.pallas_call(place, out_shape=[jax.ShapeDtypeStruct(x.shape, x.dtype) f...]
    pallas_call x1, Pallas kernels: 40.8 us -> 39.6 us  [shards(): pl.pallas_call(functools.partial(kernel, dims), out_shape=(jax.ShapeDtype...]
where the time goes in v4:
time: 41.8 us; the launch traced here: 41.6 us
  Pallas kernels  41 us (98%)
  between operations  0.64 us (2%)
    pallas_call x1, Pallas kernels, shards(): pl.pallas_call(functools.partial(kernel, dims), out_shape=(jax.ShapeDtype...  39.6 us
    pallas_call x1, Pallas kernels, shards(): pl.pallas_call(place, out_shape=[jax.ShapeDtypeStruct(x.shape, x.dtype) f...  1.39 us

profile of v4, /device:TPU:0, one launch (start us, length us, event | category | flops | bytes accessed | tf_op | source)
XLA Modules:
  0.0 41.6 jit_solution(4119447260234372912)
XLA Ops:
  0.6 39.6 %shard_map.67 = (f32[1,128]{1,0:T(1,128)}, f32[8,8,128]{2,1,0:T(8,128)}, f32[34,34]{1,0:T(8,128)}) custom-call(f32[16,128]{1,0:T(8,128)} %bitcast.11, f32[8,32,128]{2,1,0:T(8,128)} %bitcast.9, f32[8,8,128]{2,1,0:T(8,128)} %bitcast.10, f32[34,34]{1,0:T(8,128)} %core_ref.1), custom_call_target="tpu_custom_call" | custom-call | tf_op jit(solution)/shard_map/pallas_call | solution.py:276
  40.2 1.4 %shard_map.68 = (f32[1,128]{1,0:T(1,128)}, f32[8,8,128]{2,1,0:T(8,128)}, f32[34,34]{1,0:T(8,128)}) custom-call(f32[1,128]{1,0:T(1,128)} %get-tuple-element.9.refs_0_, f32[8,8,128]{2,1,0:T(8,128)} %get-tuple-element.10.refs_1_, f32[34,34]{1,0:T(8,128)} %get-tuple-element.11.refs_2_), custom_call_target="tpu_custom_call" | custom-call | tf_op jit(solution)/shard_map/pallas_call | solution.py:321

commit v5 on v4

--- a/solution.py
+++ b/solution.py
@@ -40,7 +40,8 @@
 
 def kernel(
     dims, src_ref, tgt_ref, dual_ref, core_ref, u_out, g_out, core_out,
-    srcbuf, tgtall, tgtbuf, dualbuf, corein, lsepair, lsebuf, corepair, corebuf, gbuf, sl, sr, tl, tr, sls, srs, tls, trt, sps, logits, gcol, weighted, ehigh, elow, urow, square,
+    srcbuf, tgtall, tgtbuf, dualbuf, corein, lsepair, lsebuf, corepair, corebuf, gbuf, values, lifted, sls, srs, tls, trt, logits, gcol, weighted,
+    ehigh, elow, urow, uall, turned, square,
     send_sem, recv_sem, local_sem,
 ):
     S, T, rows, cols, fs, ft, feat, ns, nt = dims
@@ -60,7 +61,7 @@
             act(lax.rem(s + k, S))
             return unused
 
-        lax.fori_loop(1, S, body, 0, unroll=S <= 8)
+        lax.fori_loop(1, S, body, 0)
 
     def remote(phase, src, dst, device):
         return pltpu.make_async_remote_copy(
@@ -96,12 +97,16 @@
     for copy in copies:
         copy.wait()
     tgtbuf[s] = tgtall[s]
-    own_dual = dualbuf[...] * (1.0 / UNIT)
-    for r in range(jr):
-        gcol[r * LANES : (r + 1) * LANES, :] = jnp.broadcast_to(own_dual[r : r + 1, :], (LANES, LANES)).T
+
+    def spread_dual(r, unused):
+        row = dualbuf[pl.ds(r, 1), :] * (1.0 / UNIT)
+        gcol[pl.ds(pl.multiple_of(r * LANES, LANES), LANES), :] = jnp.broadcast_to(row, (LANES, LANES)).T
+        return unused
+
+    lax.fori_loop(0, jr, spread_dual, 0)
     square[...] = jnp.zeros_like(square)
     square[:rank, :rank] = corein[...]
-    turned = square[...].T[:st, :]
+    turned[...] = square[...].T[:st, :]
     pl.semaphore_wait(barrier, S + T - 2)
 
     over_src(0, srcbuf.at[t])
@@ -110,13 +115,14 @@
     over_tgt(2, srcbuf)
     bytes_of(1, tgtbuf, S).wait_recv()
 
-    def lift(ref, values, ahead, scale):
-        ref[rank:, :] = jnp.zeros_like(ref[rank:, :])
+    def lift(values, ahead, scale):
         squares = jnp.sum(values * values, axis=0, keepdims=True)
         ones = jnp.ones_like(squares)
-        ref[0:1, :] = squares if ahead else ones
-        ref[1:2, :] = ones if ahead else squares
-        ref[2:rank, :] = values if scale is None else scale * values
+        lifted[rank:, :] = jnp.zeros_like(lifted[rank:, :])
+        lifted[0:1, :] = squares if ahead else ones
+        lifted[1:2, :] = ones if ahead else squares
+        lifted[2:rank, :] = values if scale is None else scale * values
+        return split3(lifted[...])
 
     def stacked(parts, height):
         width = parts[0].shape[1]
@@ -125,79 +131,102 @@
 
     deep = trt.shape[1]
     wide = srs.shape[1]
-    for k in range(S):
-        for r in range(jr):
-            tr[2 + k * ft : 2 + (k + 1) * ft, r * LANES : (r + 1) * LANES] = tgtbuf[k, r * ft : (r + 1) * ft, :]
-    lift(tr, tr[2:rank, :], False, None)
-    t0, t1, t2 = split3(tr[...])
-    trt[...] = stacked((t0, t1, t0, t1, t2, t0), deep).astype(BF16).T
-
+
+    def take_tgt(r, unused):
+        for k in range(S):
+            values[k * ft : (k + 1) * ft, :] = tgtbuf[k, r]
+        here = pl.ds(pl.multiple_of(r * LANES, LANES), LANES)
+        t0, t1, t2 = lift(values[...], False, None)
+        trt[here, :] = stacked((t0, t1, t0, t1, t2, t0), deep).astype(BF16).T
+        tls[:, here] = stacked(lift(values[...], True, -2.0), wide).astype(BF16)
+        return unused
+
+    lax.fori_loop(0, jr, take_tgt, 0)
     bytes_of(2, srcbuf, T).wait_recv()
-    for k in range(S):
-        for h in range(T):
-            sr[2 + h * fs : 2 + (h + 1) * fs, k * rows : (k + 1) * rows] = srcbuf[h, k]
-    lift(sl, sr[2:rank, :], True, -2.0)
-    sls[...] = stacked(split3(sl[...]), wide).astype(BF16)
-
+
+    def take_src(k, unused):
+        for r in range(nr):
+            for h in range(T):
+                values[h * fs : (h + 1) * fs, :] = srcbuf[h, k, :, r * LANES : (r + 1) * LANES]
+            here = pl.ds(pl.multiple_of((k * nr + r) * LANES, LANES), LANES)
+            sls[:, here] = stacked(lift(values[...], True, -2.0), wide).astype(BF16)
+            srs[here, :] = stacked(lift(values[...], False, None), wide).astype(BF16).T
+        return unused
+
+    lax.fori_loop(0, S, take_src, 0)
     per = LANES // st
     block = min(256, ns)
     chunk = min(256, cols)
-    for step in range(OUTER):
-        k0, k1, k2 = split3(turned * (-1.0 / UNIT))
+    blocks = ns // block
+
+    def outer(step, unused):
+        phase = 3 + 4 * step
+        k0, k1, k2 = split3(turned[...] * (-1.0 / UNIT))
         lhs = stacked(
             (k0 + shifted(k0, st) + shifted(k0, 2 * st), k1 + shifted(k1, st), k2), 3 * st
         ).astype(BF16)
-        proj = jnp.dot(lhs, sls[...], preferred_element_type=F32)
-        proj = proj[:st] + (proj[st : 2 * st] + proj[2 * st :])
-        p0, p1, p2 = split3(proj)
-        sps[...] = stacked((p0, p0, p1, p1, p0, p2), deep).astype(BF16)
-        for b in range(ns // block):
-            part = jnp.dot(trt[...], sps[:, b * block : (b + 1) * block], preferred_element_type=F32)
+
+        def row_block(b, unused):
+            here_b = pl.ds(pl.multiple_of(b * block, LANES), block)
+            proj = jnp.dot(lhs, sls[:, here_b], preferred_element_type=F32)
+            proj = proj[:st] + (proj[st : 2 * st] + proj[2 * st :])
+            p0, p1, p2 = split3(proj)
+            sps = stacked((p0, p0, p1, p1, p0, p2), deep).astype(BF16)
+            part = jnp.dot(trt[...], sps, preferred_element_type=F32)
             for h in range(block // LANES):
-                at = b * block // LANES + h
+                lanes_h = slice(h * LANES, (h + 1) * LANES)
                 tops, totals = [], []
                 for c in range(cols // chunk):
                     rows_c = slice(c * chunk, (c + 1) * chunk)
-                    here = part[rows_c, h * LANES : (h + 1) * LANES] + gcol[rows_c, :]
-                    logits[rows_c, at * LANES : (at + 1) * LANES] = here
+                    here = part[rows_c, lanes_h] + gcol[rows_c, :]
+                    logits[b, rows_c, lanes_h] = here
                     top = jnp.max(here, axis=0, keepdims=True)
                     tops.append(top)
                     totals.append(jnp.sum(jnp.exp2(here - top), axis=0, keepdims=True))
                 top = functools.reduce(jnp.maximum, tops)
                 total = sum(x * jnp.exp2(y - top) for x, y in zip(totals, tops))
-                lsepair[step, t, at : at + 1, :] = top + jnp.log2(total)
-        phase = 3 + 4 * step
+                lsepair[step, t, pl.ds(b * (block // LANES) + h, 1), :] = top + jnp.log2(total)
+            return unused
+
+        lax.fori_loop(0, blocks, row_block, 0)
         over_tgt(phase, lsepair.at[step])
         bytes_of(phase, lsepair.at[step], T).wait_recv()
         lsebuf[step, s] = joined(lsepair[step])
         over_src(phase + 1, lsebuf.at[step])
-        if step == 0:
-            lift(tl, tr[2:rank, :], True, -2.0)
-            tls[...] = stacked(split3(tl[...]), wide).astype(BF16)
-            lift(sr, sr[2:rank, :], False, None)
-            srs[...] = stacked(split3(sr[...]), wide).astype(BF16).T
         bytes_of(phase + 1, lsebuf.at[step], S).wait_recv()
         urow[...] = -math.log2(ns) - joined(lsebuf[step])
-        u_all = jnp.concatenate([urow[k : k + 1, :] for k in range(ns // LANES)], axis=1)
-        for c in range(cols // chunk):
-            sl_c = slice(c * chunk, (c + 1) * chunk)
-            tops = []
-            for k in range(chunk // 16):
-                x = logits[c * chunk + k * 16 : c * chunk + (k + 1) * 16, :] + u_all
-                top = jnp.max(x, axis=1, keepdims=True)
-                e = jnp.exp2(x - top)
-                high = e.astype(BF16)
-                ehigh[c, k * 16 : (k + 1) * 16, :] = high
-                elow[c, k * 16 : (k + 1) * 16, :] = (e - high.astype(F32)).astype(BF16)
-                tops.append(top)
-            top = jnp.concatenate(tops, axis=0)
-            acc = jnp.dot(ehigh[c], srs[...], preferred_element_type=F32) + jnp.dot(elow[c], srs[...], preferred_element_type=F32)
+        for k in range(ns // LANES):
+            uall[0:1, k * LANES : (k + 1) * LANES] = urow[k : k + 1, :]
+
+        def col_chunk(c, unused):
+            base = pl.multiple_of(c * chunk, chunk)
+
+            def rows_of(k, unused):
+                for n in range(4):
+                    at = pl.multiple_of(k * 64 + n * 16, 16)
+                    there = pl.ds(pl.multiple_of(base + at, 16), 16)
+                    x = jnp.concatenate([logits[b, there, :] for b in range(blocks)], axis=1) + uall[0:1, :]
+                    top = jnp.max(x, axis=1, keepdims=True)
+                    e = jnp.exp2(x - top)
+                    high = e.astype(BF16)
+                    ehigh[pl.ds(at, 16), :] = high
+                    elow[pl.ds(at, 16), :] = (e - high.astype(F32)).astype(BF16)
+                    gcol[there, :] = gcol[there, :] - top
+                return unused
+
+            lax.fori_loop(0, chunk // 64, rows_of, 0)
+            acc = jnp.dot(ehigh[...], srs[...], preferred_element_type=F32)
+            acc = acc + jnp.dot(elow[...], srs[...], preferred_element_type=F32)
             total = acc[:, 0:1]
             scaled = acc * (1.0 / total)
             first = scaled.astype(BF16)
-            weighted[sl_c, :wide] = first
-            weighted[sl_c, wide:] = (scaled - first.astype(F32)).astype(BF16)
-            gcol[sl_c, :] = (gcol[sl_c, :] - math.log2(nt)) - (top + jnp.log2(total))
+            here = pl.ds(base, chunk)
+            weighted[here, :wide] = first
+            weighted[here, wide:] = (scaled - first.astype(F32)).astype(BF16)
+            gcol[here, :] = gcol[here, :] - (math.log2(nt) + jnp.log2(total))
+            return unused
+
+        lax.fori_loop(0, cols // chunk, col_chunk, 0)
         ext = jnp.dot(tls[...], weighted[...], preferred_element_type=F32)
         ext = ext[:, :wide] + ext[:, wide:]
         kt = ext[:st] + (ext[st : 2 * st] + ext[2 * st : 3 * st])
@@ -215,21 +244,31 @@
         bytes_of(phase + 2, corepair.at[step], T).wait_recv()
         corebuf[step, s] = jnp.sum(corepair[step], axis=0)
         over_src(phase + 3, corebuf.at[step])
-        if step == OUTER - 1:
-            for r in range(jr):
-                gbuf[s, r : r + 1, :] = gcol[r * LANES : (r + 1) * LANES, :].T[0:1, :] * UNIT
+
+        @pl.when(step == OUTER - 1)
+        def finish_dual():
+            def lay(r, unused):
+                piece = gcol[pl.ds(pl.multiple_of(r * LANES, LANES), LANES), :]
+                gbuf[s, pl.ds(r, 1), :] = piece.T[0:1, :] * UNIT
+                return unused
+
+            lax.fori_loop(0, jr, lay, 0)
             over_src(last, gbuf)
+
         bytes_of(phase + 3, corebuf.at[step], S).wait_recv()
         summed = -2.0 * jnp.sum(corebuf[step], axis=0)
-        turned = jnp.concatenate(
+        turned[...] = jnp.concatenate(
             [
                 lanes_below(shifted(summed[n // per * 8 : n // per * 8 + 8, :], -(n % per) * st), st)
                 for n in range(st // 8)
             ],
             axis=0,
         )
+        return unused
+
+    lax.fori_loop(0, OUTER, outer, 0)
     u_out[...] = urow[pl.ds(s * nr, nr), :] * UNIT
-    square[:st, :] = turned
+    square[:st, :] = turned[...]
     core_out[...] = square[...].T[:rank, :rank]
 
     bytes_of(last, gbuf, S).wait_recv()
@@ -267,9 +306,9 @@
     deep = -(-6 * st // LANES) * LANES
     wide = -(-3 * st // LANES) * LANES
     dims = (S, T, rows, cols, fs, ft, feat, ns, nt)
-    chunk = min(256, cols)
+    chunk, block = min(256, cols), min(256, ns)
     src = src_feat.T
-    tgt = tgt_feat.reshape(S * jr, LANES, ft).transpose(0, 2, 1).reshape(S, jr * ft, LANES)
+    tgt = tgt_feat.reshape(S * jr, LANES, ft).transpose(0, 2, 1).reshape(S, jr, ft, LANES)
     dual = tgt_dual.reshape(S, jr, LANES)
     phases = 4 + 4 * OUTER
     vmem = pl.BlockSpec(memory_space=pltpu.VMEM)
@@ -284,8 +323,8 @@
         out_specs=(vmem,) * 3,
         scratch_shapes=[
             pltpu.VMEM((T, S, fs, rows), F32),
-            pltpu.VMEM((S, jr * ft, LANES), F32),
-            pltpu.VMEM((S, jr * ft, LANES), F32),
+            pltpu.VMEM((S, jr, ft, LANES), F32),
+            pltpu.VMEM((S, jr, ft, LANES), F32),
             pltpu.VMEM((jr, LANES), F32),
             pltpu.VMEM((rank, rank), F32),
             pltpu.VMEM((OUTER, T, ns // LANES, LANES), F32),
@@ -293,21 +332,20 @@
             pltpu.VMEM((OUTER, T, groups * 8, LANES), F32),
             pltpu.VMEM((OUTER, S, groups * 8, LANES), F32),
             pltpu.VMEM((S, jr, LANES), F32),
-            pltpu.VMEM((st, ns), F32),
-            pltpu.VMEM((st, ns), F32),
-            pltpu.VMEM((st, cols), F32),
-            pltpu.VMEM((st, cols), F32),
+            pltpu.VMEM((feat, LANES), F32),
+            pltpu.VMEM((st, LANES), F32),
             pltpu.VMEM((wide, ns), BF16),
             pltpu.VMEM((ns, wide), BF16),
             pltpu.VMEM((wide, cols), BF16),
             pltpu.VMEM((cols, deep), BF16),
-            pltpu.VMEM((deep, ns), BF16),
-            pltpu.VMEM((cols, ns), F32),
+            pltpu.VMEM((ns // block, cols, block), F32),
             pltpu.VMEM((cols, LANES), F32),
             pltpu.VMEM((cols, 2 * wide), BF16),
-            pltpu.VMEM((cols // chunk, chunk, ns), BF16),
-            pltpu.VMEM((cols // chunk, chunk, ns), BF16),
+            pltpu.VMEM((chunk, ns), BF16),
+            pltpu.VMEM((chunk, ns), BF16),
             pltpu.VMEM((ns // LANES, LANES), F32),
+            pltpu.VMEM((1, ns), F32),
+            pltpu.VMEM((st, LANES), F32),
             pltpu.VMEM((LANES, LANES), F32),
             pltpu.SemaphoreType.DMA((phases,)),
             pltpu.SemaphoreType.DMA((phases,)),

time: 41.8 us -> 49.9 us (1.19)
  Pallas kernels: 41 us -> 49.1 us
    pallas_call x1, Pallas kernels: 39.6 us -> 47.7 us  [shards(): pl.pallas_call(functools.partial(kernel, dims), out_shape=(jax.ShapeDtype...]
where the time goes in v5:
time: 49.9 us; the launch traced here: 49.7 us
  Pallas kernels  49.1 us (98%)
  between operations  0.64 us (1%)
    pallas_call x1, Pallas kernels, shards(): pl.pallas_call(functools.partial(kernel, dims), out_shape=(jax.ShapeDtype...  47.7 us
    pallas_call x1, Pallas kernels, shards(): pl.pallas_call(place, out_shape=[jax.ShapeDtypeStruct(x.shape, x.dtype) f...  1.39 us

profile of v5, /device:TPU:0, one launch (start us, length us, event | category | flops | bytes accessed | tf_op | source)
XLA Modules:
  0.0 49.7 jit_solution(17096803070926225464)
XLA Ops:
  0.6 47.7 %shard_map.67 = (f32[1,128]{1,0:T(1,128)}, f32[8,8,128]{2,1,0:T(8,128)}, f32[34,34]{1,0:T(8,128)}) custom-call(f32[16,128]{1,0:T(8,128)} %bitcast.11, f32[8,8,4,128]{3,2,1,0:T(4,128)} %bitcast.9, f32[8,8,128]{2,1,0:T(8,128)} %bitcast.10, f32[34,34]{1,0:T(8,128)} %core_ref.1), custom_call_target="tpu_custom_call" | custom-call | tf_op jit(solution)/shard_map/pallas_call | solution.py:315
  48.3 1.4 %shard_map.68 = (f32[1,128]{1,0:T(1,128)}, f32[8,8,128]{2,1,0:T(8,128)}, f32[34,34]{1,0:T(8,128)}) custom-call(f32[1,128]{1,0:T(1,128)} %get-tuple-element.9.refs_0_, f32[8,8,128]{2,1,0:T(8,128)} %get-tuple-element.10.refs_1_, f32[34,34]{1,0:T(8,128)} %get-tuple-element.11.refs_2_), custom_call_target="tpu_custom_call" | custom-call | tf_op jit(solution)/shard_map/pallas_call | solution.py:359

commit v6 on v4

--- a/solution.py
+++ b/solution.py
@@ -40,7 +40,7 @@
 
 def kernel(
     dims, src_ref, tgt_ref, dual_ref, core_ref, u_out, g_out, core_out,
-    srcbuf, tgtall, tgtbuf, dualbuf, corein, lsepair, lsebuf, corepair, corebuf, gbuf, sl, sr, tl, tr, sls, srs, tls, trt, sps, logits, gcol, weighted, ehigh, elow, urow, square,
+    srcbuf, tgtall, tgtbuf, dualbuf, corein, lsepair, lsebuf, corepair, corebuf, gbuf, sl, sr, tl, tr, sls, srs, tls, trt, sps, logits, gcol, weighted, ehigh, elow, urow, turned, square,
     send_sem, recv_sem, local_sem,
 ):
     S, T, rows, cols, fs, ft, feat, ns, nt = dims
@@ -101,7 +101,7 @@
         gcol[r * LANES : (r + 1) * LANES, :] = jnp.broadcast_to(own_dual[r : r + 1, :], (LANES, LANES)).T
     square[...] = jnp.zeros_like(square)
     square[:rank, :rank] = corein[...]
-    turned = square[...].T[:st, :]
+    turned[...] = square[...].T[:st, :]
     pl.semaphore_wait(barrier, S + T - 2)
 
     over_src(0, srcbuf.at[t])
@@ -142,8 +142,8 @@
     per = LANES // st
     block = min(256, ns)
     chunk = min(256, cols)
-    for step in range(OUTER):
-        k0, k1, k2 = split3(turned * (-1.0 / UNIT))
+    def outer(step, unused):
+        k0, k1, k2 = split3(turned[...] * (-1.0 / UNIT))
         lhs = stacked(
             (k0 + shifted(k0, st) + shifted(k0, 2 * st), k1 + shifted(k1, st), k2), 3 * st
         ).astype(BF16)
@@ -151,45 +151,52 @@
         proj = proj[:st] + (proj[st : 2 * st] + proj[2 * st :])
         p0, p1, p2 = split3(proj)
         sps[...] = stacked((p0, p0, p1, p1, p0, p2), deep).astype(BF16)
+        sublogs = []
         for b in range(ns // block):
             part = jnp.dot(trt[...], sps[:, b * block : (b + 1) * block], preferred_element_type=F32)
             for h in range(block // LANES):
                 at = b * block // LANES + h
-                tops, totals = [], []
+                tops = []
                 for c in range(cols // chunk):
                     rows_c = slice(c * chunk, (c + 1) * chunk)
                     here = part[rows_c, h * LANES : (h + 1) * LANES] + gcol[rows_c, :]
                     logits[rows_c, at * LANES : (at + 1) * LANES] = here
-                    top = jnp.max(here, axis=0, keepdims=True)
-                    tops.append(top)
-                    totals.append(jnp.sum(jnp.exp2(here - top), axis=0, keepdims=True))
+                    tops.append(jnp.max(here.reshape(chunk // 8, 8, LANES), axis=0))
                 top = functools.reduce(jnp.maximum, tops)
-                total = sum(x * jnp.exp2(y - top) for x, y in zip(totals, tops))
-                lsepair[step, t, at : at + 1, :] = top + jnp.log2(total)
+                totals = []
+                for c in range(cols // chunk):
+                    here = logits[c * chunk : (c + 1) * chunk, at * LANES : (at + 1) * LANES]
+                    totals.append(jnp.sum(jnp.exp2(here.reshape(chunk // 8, 8, LANES) - top[None]), axis=0))
+                sublogs.append(top + jnp.log2(sum(totals)))
+        for at in range(ns // LANES):
+            top = jnp.max(sublogs[at], axis=0, keepdims=True)
+            total = jnp.sum(jnp.exp2(sublogs[at] - top), axis=0, keepdims=True)
+            lsepair[step, t, at : at + 1, :] = top + jnp.log2(total)
         phase = 3 + 4 * step
         over_tgt(phase, lsepair.at[step])
         bytes_of(phase, lsepair.at[step], T).wait_recv()
         lsebuf[step, s] = joined(lsepair[step])
         over_src(phase + 1, lsebuf.at[step])
-        if step == 0:
+
+        @pl.when(step == 0)
+        def prepare():
             lift(tl, tr[2:rank, :], True, -2.0)
             tls[...] = stacked(split3(tl[...]), wide).astype(BF16)
             lift(sr, sr[2:rank, :], False, None)
             srs[...] = stacked(split3(sr[...]), wide).astype(BF16).T
+
         bytes_of(phase + 1, lsebuf.at[step], S).wait_recv()
         urow[...] = -math.log2(ns) - joined(lsebuf[step])
         u_all = jnp.concatenate([urow[k : k + 1, :] for k in range(ns // LANES)], axis=1)
         for c in range(cols // chunk):
             sl_c = slice(c * chunk, (c + 1) * chunk)
-            tops = []
-            for k in range(chunk // 16):
-                x = logits[c * chunk + k * 16 : c * chunk + (k + 1) * 16, :] + u_all
-                top = jnp.max(x, axis=1, keepdims=True)
-                e = jnp.exp2(x - top)
+            starts = range(c * chunk, (c + 1) * chunk, 16)
+            tops = [jnp.max(logits[k : k + 16, :] + u_all, axis=1, keepdims=True) for k in starts]
+            for k, top in zip(starts, tops):
+                e = jnp.exp2((logits[k : k + 16, :] + u_all) - top)
                 high = e.astype(BF16)
-                ehigh[c, k * 16 : (k + 1) * 16, :] = high
-                elow[c, k * 16 : (k + 1) * 16, :] = (e - high.astype(F32)).astype(BF16)
-                tops.append(top)
+                ehigh[c, k - c * chunk : k - c * chunk + 16, :] = high
+                elow[c, k - c * chunk : k - c * chunk + 16, :] = (e - high.astype(F32)).astype(BF16)
             top = jnp.concatenate(tops, axis=0)
             acc = jnp.dot(ehigh[c], srs[...], preferred_element_type=F32) + jnp.dot(elow[c], srs[...], preferred_element_type=F32)
             total = acc[:, 0:1]
@@ -215,21 +222,27 @@
         bytes_of(phase + 2, corepair.at[step], T).wait_recv()
         corebuf[step, s] = jnp.sum(corepair[step], axis=0)
         over_src(phase + 3, corebuf.at[step])
-        if step == OUTER - 1:
+
+        @pl.when(step == OUTER - 1)
+        def finish_dual():
             for r in range(jr):
                 gbuf[s, r : r + 1, :] = gcol[r * LANES : (r + 1) * LANES, :].T[0:1, :] * UNIT
             over_src(last, gbuf)
+
         bytes_of(phase + 3, corebuf.at[step], S).wait_recv()
         summed = -2.0 * jnp.sum(corebuf[step], axis=0)
-        turned = jnp.concatenate(
+        turned[...] = jnp.concatenate(
             [
                 lanes_below(shifted(summed[n // per * 8 : n // per * 8 + 8, :], -(n % per) * st), st)
                 for n in range(st // 8)
             ],
             axis=0,
         )
+        return unused
+
+    lax.fori_loop(0, OUTER, outer, 0)
     u_out[...] = urow[pl.ds(s * nr, nr), :] * UNIT
-    square[:st, :] = turned
+    square[:st, :] = turned[...]
     core_out[...] = square[...].T[:rank, :rank]
 
     bytes_of(last, gbuf, S).wait_recv()
@@ -308,6 +321,7 @@
             pltpu.VMEM((cols // chunk, chunk, ns), BF16),
             pltpu.VMEM((cols // chunk, chunk, ns), BF16),
             pltpu.VMEM((ns // LANES, LANES), F32),
+            pltpu.VMEM((st, LANES), F32),
             pltpu.VMEM((LANES, LANES), F32),
             pltpu.SemaphoreType.DMA((phases,)),
             pltpu.SemaphoreType.DMA((phases,)),

time: 41.8 us -> 42.1 us (level)
  no operation moved by 1% of the time
where the time goes in v6:
time: 42.1 us; the launch traced here: 41.9 us
  Pallas kernels  41.2 us (98%)
  between operations  0.64 us (2%)
    pallas_call x1, Pallas kernels, shards(): pl.pallas_call(functools.partial(kernel, dims), out_shape=(jax.ShapeDtype...  39.8 us
    pallas_call x1, Pallas kernels, shards(): pl.pallas_call(place, out_shape=[jax.ShapeDtypeStruct(x.shape, x.dtype) f...  1.39 us

profile of v6, /device:TPU:0, one launch (start us, length us, event | category | flops | bytes accessed | tf_op | source)
XLA Modules:
  0.0 41.9 jit_solution(11702318308964106070)
XLA Ops:
  0.6 39.8 %shard_map.67 = (f32[1,128]{1,0:T(1,128)}, f32[8,8,128]{2,1,0:T(8,128)}, f32[34,34]{1,0:T(8,128)}) custom-call(f32[16,128]{1,0:T(8,128)} %bitcast.11, f32[8,32,128]{2,1,0:T(8,128)} %bitcast.9, f32[8,8,128]{2,1,0:T(8,128)} %bitcast.10, f32[34,34]{1,0:T(8,128)} %core_ref.1), custom_call_target="tpu_custom_call" | custom-call | tf_op jit(solution)/shard_map/pallas_call | solution.py:289
  40.5 1.4 %shard_map.68 = (f32[1,128]{1,0:T(1,128)}, f32[8,8,128]{2,1,0:T(8,128)}, f32[34,34]{1,0:T(8,128)}) custom-call(f32[1,128]{1,0:T(1,128)} %get-tuple-element.9.refs_0_, f32[8,8,128]{2,1,0:T(8,128)} %get-tuple-element.10.refs_1_, f32[34,34]{1,0:T(8,128)} %get-tuple-element.11.refs_2_), custom_call_target="tpu_custom_call" | custom-call | tf_op jit(solution)/shard_map/pallas_call | solution.py:335

commit v7 on v6

--- a/solution.py
+++ b/solution.py
@@ -141,7 +141,7 @@
 
     per = LANES // st
     block = min(256, ns)
-    chunk = min(256, cols)
+    chunk = min(512, cols)
     def outer(step, unused):
         k0, k1, k2 = split3(turned[...] * (-1.0 / UNIT))
         lhs = stacked(
@@ -280,7 +280,7 @@
     deep = -(-6 * st // LANES) * LANES
     wide = -(-3 * st // LANES) * LANES
     dims = (S, T, rows, cols, fs, ft, feat, ns, nt)
-    chunk = min(256, cols)
+    chunk = min(512, cols)
     src = src_feat.T
     tgt = tgt_feat.reshape(S * jr, LANES, ft).transpose(0, 2, 1).reshape(S, jr * ft, LANES)
     dual = tgt_dual.reshape(S, jr, LANES)

time: 42.1 us -> 42.5 us (level)
  no operation moved by 1% of the time
where the time goes in v7:
time: 42.5 us; the launch traced here: 42.3 us
  Pallas kernels  41.6 us (98%)
  between operations  0.64 us (2%)
    pallas_call x1, Pallas kernels, shards(): pl.pallas_call(functools.partial(kernel, dims), out_shape=(jax.ShapeDtype...  40.2 us
    pallas_call x1, Pallas kernels, shards(): pl.pallas_call(place, out_shape=[jax.ShapeDtypeStruct(x.shape, x.dtype) f...  1.39 us

profile of v7, /device:TPU:0, one launch (start us, length us, event | category | flops | bytes accessed | tf_op | source)
XLA Modules:
  0.0 42.3 jit_solution(13031001636771032980)
XLA Ops:
  0.6 40.2 %shard_map.67 = (f32[1,128]{1,0:T(1,128)}, f32[8,8,128]{2,1,0:T(8,128)}, f32[34,34]{1,0:T(8,128)}) custom-call(f32[16,128]{1,0:T(8,128)} %bitcast.11, f32[8,32,128]{2,1,0:T(8,128)} %bitcast.9, f32[8,8,128]{2,1,0:T(8,128)} %bitcast.10, f32[34,34]{1,0:T(8,128)} %core_ref.1), custom_call_target="tpu_custom_call" | custom-call | tf_op jit(solution)/shard_map/pallas_call | solution.py:289
  40.9 1.4 %shard_map.68 = (f32[1,128]{1,0:T(1,128)}, f32[8,8,128]{2,1,0:T(8,128)}, f32[34,34]{1,0:T(8,128)}) custom-call(f32[1,128]{1,0:T(1,128)} %get-tuple-element.9.refs_0_, f32[8,8,128]{2,1,0:T(8,128)} %get-tuple-element.10.refs_1_, f32[34,34]{1,0:T(8,128)} %get-tuple-element.11.refs_2_), custom_call_target="tpu_custom_call" | custom-call | tf_op jit(solution)/shard_map/pallas_call | solution.py:335
